TPU v7x, 512 devices: a whole 4x8x8 slice. The times are simulated.
512 devices in a mesh: fsdp: 128 (over z, y, core), tp: 4 (over x).
Axes of the slice: x: 4, y: 8, z: 8, core: 2. Of those that a mesh axis runs over, the one named last changes fastest.
Arguments:
- hidden_rows: bfloat16 [32768, 5120], P('fsdp', 'tp'), may hold values from -6 to 6
- cotangent: bfloat16 [32768, 2560], P('fsdp', 'tp'), may hold values from -6 to 6
- norm_gain: float32 [5120], replicated, may hold values from 0.1 to 1.9
- query_weight: bfloat16 [5120, 2560], P('fsdp', 'tp'), may hold values from -4 to 4
- key_weight: bfloat16 [5120, 512], P('fsdp', 'tp'), may hold values from -4 to 4
- value_weight: bfloat16 [5120, 512], P('fsdp', 'tp'), may hold values from -0.078125 to 0.078125
- slot_source: int32 [512], P('fsdp'), may hold values from -1 to 3, as said below
- slot_segment: int32 [512], P('fsdp'), may hold values from -1 to 255, as said below
- slot_position: int32 [512], P('fsdp'), may hold values from 0 to 1, as said below
Outputs:
- attended: bfloat16 [32768, 2560], P('fsdp', 'tp')
- value_grad: float32 [5120, 512], P('fsdp', 'tp')
Inputs may be any that keep to these rules, and one draw needn't show every extreme that they name: `slot_source`: -1 marks an empty slot; c < 2 names block c of the learner's own fsdp index, c >= 2 block c - 2 of the index before it (cyclically). Each block is held by at most one slot; some learner has all 4 slots filled; all blocks of one sequence stand on one learner. `slot_segment`: each sequence has one id, unique over the whole rollout (the fsdp index that produced it times 2 plus its first block); -1 marks an empty slot; the largest id occurs in every draw. `slot_position`: the blocks of one sequence have the positions 0, 1, 2 and so on, each once; 0 in an empty slot.
All inputs are finite; a program needn't handle non-finite values.
Results may differ from a plain program's by a relative error of at most 0.0079.
Values may be sent and summed in bfloat16 or wider, within the bound.
A program may use at most 64 MiB of HBM per device.

v0:
```python
import jax
import jax.numpy as jnp
from jax import lax
from jax.sharding import PartitionSpec as P

HD = 128
BLK = 128
GEN_BLK = 2
CAP_BLK = 4


epsilon = 1e-06


def passed_along(value, axis, steps):
    count = lax.axis_size(axis)
    pairs = [(source, (source + steps) % count) for source in range(count)]
    return lax.ppermute(value, axis, pairs)


def place_rows(stacked, source):
    filled = source >= 0
    picked = jnp.take(stacked, jnp.maximum(source, 0), axis=0)
    return jnp.where(filled[:, None, None], picked, jnp.zeros_like(picked))


def norm_rows(whole, norm_gain):
    wide_rows = whole.astype(jnp.float32)
    mean_sq = jnp.mean(wide_rows * wide_rows, axis=1, keepdims=True)
    return (wide_rows * lax.rsqrt(mean_sq + epsilon) * norm_gain).astype(jnp.bfloat16)


def shards(
    hidden_rows,
    cotangent,
    norm_gain,
    query_weight,
    key_weight,
    value_weight,
    slot_source,
    slot_segment,
    slot_position,
):
    width_part = cotangent.shape[1]
    group = width_part // HD
    slot_rows = CAP_BLK * BLK

    def to_slots(own_rows, prev_rows):
        stacked = jnp.concatenate(
            [own_rows.reshape(GEN_BLK, BLK, -1), prev_rows.reshape(GEN_BLK, BLK, -1)], axis=0
        )
        return place_rows(stacked, slot_source).reshape(slot_rows, -1)

    rows_prev, cot_prev = passed_along((hidden_rows, cotangent), "fsdp", 1)
    narrow = to_slots(hidden_rows, rows_prev)
    whole = lax.all_gather(narrow, "tp", axis=1, tiled=True)
    cot_slots = to_slots(cotangent, cot_prev).reshape(slot_rows, group, HD)
    normed = norm_rows(whole, norm_gain)

    def add_piece(piece):
        return jnp.dot(normed, piece, preferred_element_type=jnp.float32)

    query_sum = add_piece(lax.all_gather(query_weight, "fsdp", axis=0, tiled=True))
    key_sum = add_piece(lax.all_gather(key_weight, "fsdp", axis=0, tiled=True))
    value_sum = add_piece(lax.all_gather(value_weight, "fsdp", axis=0, tiled=True))
    queries = query_sum.astype(jnp.bfloat16)
    keys = key_sum.astype(jnp.bfloat16)
    values = value_sum.astype(jnp.bfloat16)
    queries = queries.reshape(slot_rows, group, HD)
    inside = jnp.arange(BLK, dtype=jnp.int32)
    fill_tok = jnp.repeat(slot_source >= 0, BLK)
    seg_tok = jnp.repeat(slot_segment, BLK)
    pos_tok = jnp.repeat(slot_position, BLK) * BLK + jnp.tile(inside, CAP_BLK)
    allow = (
        fill_tok[:, None]
        & fill_tok[None, :]
        & (seg_tok[:, None] == seg_tok[None, :])
        & (pos_tok[:, None] >= pos_tok[None, :])
    )
    scores = jnp.einsum("qgd,kd->gqk", queries, keys, preferred_element_type=jnp.float32) * HD ** (
        -0.5
    )
    masked = jnp.where(allow[None], scores, -1e30)
    row_max = jnp.max(masked, axis=2, keepdims=True)
    raised = jnp.where(allow[None], jnp.exp(masked - row_max), 0.0)
    denom = (
        jnp.sum(raised, axis=2, keepdims=True) + (1.0 - fill_tok.astype(jnp.float32))[None, :, None]
    )
    probs = (raised / denom).astype(jnp.bfloat16)
    out_slots = jnp.einsum("gqk,kd->qgd", probs, values, preferred_element_type=jnp.float32).astype(
        jnp.bfloat16
    )
    out_slots = out_slots.reshape(CAP_BLK, BLK, width_part)
    value_cot = jnp.einsum(
        "gqk,qgd->kd", probs, cot_slots, preferred_element_type=jnp.float32
    ).astype(jnp.bfloat16)
    candidates = jnp.arange(2 * GEN_BLK, dtype=jnp.int32)
    matches = slot_source[None, :] == candidates[:, None]
    named = jnp.any(matches, axis=1)
    which_slot = jnp.sum(
        jnp.where(matches, jnp.arange(CAP_BLK, dtype=jnp.int32)[None, :], 0), axis=1
    )
    anchor_slot = jnp.where(named, which_slot, -1)
    back_rows = place_rows(out_slots, anchor_slot)
    returned = passed_along(back_rows[GEN_BLK:], "fsdp", -1)
    attended = (back_rows[:GEN_BLK] + returned).reshape(GEN_BLK * BLK, width_part)
    value_grad = lax.psum_scatter(
        lax.dot_general(
            normed, value_cot, (((0,), (0,)), ((), ())), preferred_element_type=jnp.float32
        ),
        "fsdp",
        scatter_dimension=0,
        tiled=True,
    )
    return (attended, value_grad)


def solution(mesh):
    return jax.shard_map(
        shards,
        mesh=mesh,
        in_specs=(
            P("fsdp", "tp"),
            P("fsdp", "tp"),
            P(),
            P("fsdp", "tp"),
            P("fsdp", "tp"),
            P("fsdp", "tp"),
            P("fsdp"),
            P("fsdp"),
            P("fsdp"),
        ),
        out_specs=(P("fsdp", "tp"), P("fsdp", "tp")),
        check_vma=False,
    )
```

profile of v0, /device:TPU:1, one launch (start us, length us, event | category | flops | bytes accessed | tf_op | source)
XLA Modules:
  0.0 544.6 jit_solution(4352852762398062409)
XLA Ops:
  7.2 4.7 collective-permute-start
  12.0 0.7 broadcast_maximum_fusion.1
  12.6 0.7 broadcast_compare_fusion.2
  13.3 0.1 broadcast_bitcast_fusion.2
  13.4 0.1 broadcast_bitcast_fusion.1
  13.5 6.3 %collective-permute-done = bf16[256,1280]{1,0:T(8,128)(2,1)S(1)} collective-permute-done((bf16[256,1280]{1,0:T(8,128)(2,1)}, bf16[256,1280]{1,0:T(8,128)(2,1)S(1)}, u32[]{:S(2)}, u32[]{:S(2)}) %collective-permute-start) | collective-permute-done | bytes 655392 | tf_op jit(solution)/shard_map/ppermute | solution.py:18
  19.8 1.2 pad_maximum_fusion
  21.0 0.6 gather_fusion
  21.6 1.4 fusion.8
  23.0 0.0 all-gather.11.cloned.1.call-start
  23.1 0.7 all-gather.11.cloned.1.call-update
  23.8 0.0 all-gather.9.cloned.1.call-start
  23.8 0.7 all-gather.9.cloned.1.call-update
  24.5 0.0 all-gather.7.cloned.1.call-start
  24.6 4.3 collective-permute-start.2
  28.9 0.0 reduce-scatter.4.cloned.1.call-start
  29.0 0.1 add_bitcast_fusion
  29.0 0.1 convert_subtract_fusion
  29.1 0.4 compare_and_fusion
  29.5 8.9 %collective-permute-done.2 = bf16[256,640]{1,0:T(8,128)(2,1)S(1)} collective-permute-done((bf16[256,640]{1,0:T(8,128)(2,1)S(1)}, bf16[256,640]{1,0:T(8,128)(2,1)S(1)}, u32[]{:S(2)}, u32[]{:S(2)}) %collective-permute-start.2) | collective-permute-done | bytes 327712 | tf_op jit(solution)/shard_map/ppermute | solution.py:18
  38.4 0.1 pad_maximum_fusion.1
  38.5 0.7 gather_fusion.2
  39.2 0.2 select_select_fusion
  39.3 1.7 reshape.242
  41.0 50.8 %all-gather.5.cloned.1.call-done = bf16[512,5120]{1,0:T(8,128)(2,1)} async-done(((bf16[512,1280]{1,0:T(8,128)(2,1)}), bf16[512,5120]{1,0:T(8,128)(2,1)}) %all-gather.5.cloned.1.call-update) | async-done | bytes 5242896 | tf_op jit(solution)/shard_map/all_gather | solution.py:56
  91.8 3.7 fusion.1
  95.6 0.3 copy-done
  95.9 4.4 fusion.3
  100.3 82.5 %all-gather.11.cloned.1.call-done = bf16[5120,640]{1,0:T(8,128)(2,1)} async-done(((bf16[40,640]{1,0:T(8,128)(2,1)}), bf16[5120,640]{1,0:T(8,128)(2,1)}) %all-gather.11.cloned.1.call-update) | async-done | bytes 6553616 | tf_op jit(solution)/shard_map/all_gather | solution.py:63
  182.8 8.6 %convolution_convert_fusion.1 = bf16[512,640]{1,0:T(8,128)(2,1)S(1)} fusion(bf16[512,5120]{1,0:T(8,128)(2,1)} %fusion.3, bf16[5120,640]{1,0:T(8,128)(2,1)} %all-gather.11.cloned.1.call-done), kind=kOutput, calls=%fused_computation.17 | convolution fusion | flops 3355770880 | bytes 12451840 | tf_op jit(solution)/shard_map/dot_general | solution.py:61
  191.4 0.3 copy.32
  191.7 73.4 %all-gather.9.cloned.1.call-done = bf16[5120,128]{1,0:T(8,128)(2,1)} async-done(((bf16[40,128]{1,0:T(8,128)(2,1)}), bf16[5120,128]{1,0:T(8,128)(2,1)}) %all-gather.9.cloned.1.call-update) | async-done | bytes 1310736 | tf_op jit(solution)/shard_map/all_gather | solution.py:64
  265.0 8.7 %fusion.14 = f32[512,512,5]{1,0,2:T(8,128)} fusion(bf16[512,5,128]{0,2,1:T(8,128)(2,1)S(1)} %bitcast.59, bf16[512,5120]{1,0:T(8,128)(2,1)} %fusion.3, bf16[5120,128]{1,0:T(8,128)(2,1)} %all-gather.9.cloned.1.call-done), kind=kOutput, calls=%fused_computation.29 | convolution fusion | flops 1006698496 | bytes 12451840 | tf_op jit(solution)/shard_map/qgd,kd->gqk/dot_general | solution.py:80
  273.7 6.9 %fusion.20 = (f32[5,512]{1,0:T(8,128)S(1)}, f32[5,512,512]{1,2,0:T(8,128)S(1)}) fusion(f32[512,512,5]{1,0,2:T(8,128)} %fusion.14, pred[512,512]{0,1:T(8,128)(4,1)S(1)} %compare_and_fusion), kind=kOutput, calls=%fused_computation.58 | output fusion | flops 9175551 | bytes 10758144 | tf_op jit(solution)/shard_map/sub | solution.py:85
  280.6 0.8 divide_convert_fusion
  281.4 7.9 %fusion.11 = f32[5120,128]{1,0:T(8,128)} fusion(bf16[512,5120]{1,0:T(8,128)(2,1)} %fusion.3, bf16[5,512,512]{1,2,0:T(8,128)(2,1)S(1)} %divide_convert_fusion, bf16[512,5,128]{2,1,0:T(8,128)(2,1)} %reshape.242), kind=kOutput, calls=%fused_computation.26 | convolution fusion | flops 1006698496 | bytes 11141120 | tf_op jit(solution)/shard_map/dot_general | solution.py:108
  289.4 0.1 fusion.17
  289.5 0.1 select_reduce_fusion
  289.6 57.7 %all-gather.7.cloned.1.call-done = bf16[5120,128]{1,0:T(8,128)(2,1)} async-done(((bf16[40,128]{1,0:T(8,128)(2,1)}), bf16[5120,128]{1,0:T(8,128)(2,1)}) %all-gather.7.cloned.1.call-update) | async-done | bytes 1310736 | tf_op jit(solution)/shard_map/all_gather | solution.py:65
  347.3 5.5 %fusion.9 = bf16[512,5,128]{0,2,1:T(8,128)(2,1)S(1)} fusion(bf16[5,512,512]{1,2,0:T(8,128)(2,1)S(1)} %divide_convert_fusion, bf16[512,5120]{1,0:T(8,128)(2,1)} %fusion.3, bf16[5120,128]{1,0:T(8,128)(2,1)} %all-gather.7.cloned.1.call-done), kind=kOutput, calls=%fused_computation.21 | convolution fusion | flops 1007026176 | bytes 9830400 | tf_op jit(solution)/shard_map/gqk,kd->qgd/dot_general | solution.py:90
  352.9 0.2 reshape.204
  353.0 0.9 copy.36
  353.9 0.7 gather_fusion.1
  354.6 0.2 select_select_fusion.1
  354.8 2.2 collective-permute-start.1
  356.9 6.2 %collective-permute-done.1 = bf16[2,128,640]{2,1,0:T(8,128)(2,1)S(1)} collective-permute-done((bf16[2,128,640]{2,1,0:T(8,128)(2,1)S(1)}, bf16[2,128,640]{2,1,0:T(8,128)(2,1)S(1)}, u32[]{:S(2)}, u32[]{:S(2)}) %collective-permute-start.1) | collective-permute-done | bytes 327712 | tf_op jit(solution)/shard_map/ppermute | solution.py:18
  363.2 0.8 slice_add_fusion
  364.0 174.1 %reduce-scatter.4.cloned.1.call-done = f32[40,128]{1,0:T(8,128)} async-done(((f32[5120,128]{1,0:T(8,128)}), f32[40,128]{1,0:T(8,128)}) %reduce-scatter.4.cloned.1.call-update) | async-done | bytes 20496
  (22 shorter events, 0.2 us)
Async XLA Ops:
  7.2 17.4 %copy-start.1 = (bf16[256,640]{1,0:T(8,128)(2,1)S(1)}, bf16[256,640]{1,0:T(8,128)(2,1)}, u32[]{:S(2)}) copy-start(bf16[256,640]{1,0:T(8,128)(2,1)} %param.12) | copy-start | bytes 983044
  7.2 21.8 %copy-start.4 = (s32[4]{0:T(128)S(1)}, s32[4]{0:T(128)}, u32[]{:S(2)}) copy-start(s32[4]{0:T(128)} %param.19) | copy-start | bytes 52
  7.2 21.8 %copy-start.3 = (s32[4]{0:T(128)S(1)}, s32[4]{0:T(128)}, u32[]{:S(2)}) copy-start(s32[4]{0:T(128)} %param.18) | copy-start | bytes 52
  7.2 84.6 %all-gather.5.cloned.1.call-start = ((), (), s32[]{:S(2)}) async-start(), calls=%async_computation.1 | async-start | bytes 6553600 | tf_op jit(solution)/shard_map/all_gather | solution.py:56
  7.2 12.6 %collective-permute-start = (bf16[256,1280]{1,0:T(8,128)(2,1)}, bf16[256,1280]{1,0:T(8,128)(2,1)S(1)}, u32[]{:S(2)}, u32[]{:S(2)}) collective-permute-start(bf16[256,1280]{1,0:T(8,128)(2,1)} %param.11), channel_id=1, source_target_pairs={{0,4},{4,8},{8,12},{12,16},{16,20},{20,24},{24,28},{28,32},{32,36}... | collective-permute-start | bytes 1966088 | tf_op jit(solution)/shard_map/ppermute | solution.py:18
  23.0 159.8 %all-gather.11.cloned.1.call-start = ((), (), s32[]{:S(2)}) async-start(), calls=%async_computation.4 | async-start | bytes 6604800 | tf_op jit(solution)/shard_map/all_gather | solution.py:63
  23.8 241.3 %all-gather.9.cloned.1.call-start = ((), (), s32[]{:S(2)}) async-start(), calls=%async_computation.3 | async-start | bytes 1320960 | tf_op jit(solution)/shard_map/all_gather | solution.py:64
  24.5 322.8 %all-gather.7.cloned.1.call-start = ((), (), s32[]{:S(2)}) async-start(), calls=%async_computation.2 | async-start | bytes 1320960 | tf_op jit(solution)/shard_map/all_gather | solution.py:65
  24.6 13.9 %collective-permute-start.2 = (bf16[256,640]{1,0:T(8,128)(2,1)S(1)}, bf16[256,640]{1,0:T(8,128)(2,1)S(1)}, u32[]{:S(2)}, u32[]{:S(2)}) collective-permute-start(bf16[256,640]{1,0:T(8,128)(2,1)S(1)} %copy-done.1), channel_id=1, source_target_pairs={{0,4},{4,8},{8,12},{12,16},{16,20},{20,24},{24,28},{28,32},{32,36}... | collective-permute-start | bytes 983048 | tf_op jit(solution)/shard_map/ppermute | solution.py:18
  28.9 509.2 %reduce-scatter.4.cloned.1.call-start = ((), (), s32[]{:S(2)}) async-start(), calls=%async_computation.5 | async-start | bytes 2641920
  38.4 57.1 %copy-start.2 = (f32[5120]{0:T(1024)S(1)}, f32[5120]{0:T(1024)}, u32[]{:S(2)}) copy-start(f32[5120]{0:T(1024)} %param.13) | copy-start | bytes 61444
  91.8 4.0 copy-start
  281.4 7.9 %copy-start.5 = (s32[4]{0:T(128)S(1)}, s32[4]{0:T(128)}, u32[]{:S(2)}) copy-start(s32[4]{0:T(128)} %param.17) | copy-start | bytes 52
  354.8 8.4 %collective-permute-start.1 = (bf16[2,128,640]{2,1,0:T(8,128)(2,1)S(1)}, bf16[2,128,640]{2,1,0:T(8,128)(2,1)S(1)}, u32[]{:S(2)}, u32[]{:S(2)}) collective-permute-start(bf16[2,128,640]{2,1,0:T(8,128)(2,1)S(1)} %slice.15), channel_id=1, source_target_pairs={{0,508},{4,0},{8,4},{12,8},{16,12},{20,16},{24,20},{28,24},{32,28}... | collective-permute-start | bytes 983048 | tf_op jit(solution)/shard_map/ppermute | solution.py:18
Sparse Core Ops, SparseCore 0:
  23.1 68.6 all-gather.4
  95.0 87.7 all-gather.10
  186.0 79.0 all-gather.8
  268.1 79.2 all-gather.6
  352.2 185.8 reduce-scatter.3
where the time goes:
time: 549 us; the launch traced here: 545 us
  waiting for transfers between devices  461 us (84%)
  matrix products  30.7 us (6%)
  other arithmetic  21.6 us (4%)
  between operations  14 us (3%)
  starting transfers between devices  11.4 us (2%)
    unnamed x6, waiting for transfers between devices  176 us
    all_gather x1, waiting for transfers between devices, shards(): lax.all_gather(query_weight, 'fsdp', axis=0, tiled=True)  82.5 us
    all_gather x1, waiting for transfers between devices, shards(): key_sum = add_piece(lax.all_gather(key_weight, 'fsdp', axis=0, tiled=True))  73.4 us
    all_gather x1, waiting for transfers between devices, shards(): lax.all_gather(value_weight, 'fsdp', axis=0, tiled=True)  57.7 us
    all_gather x1, waiting for transfers between devices, shards(): whole = lax.all_gather(narrow, 'tp', axis=1, tiled=True)  50.8 us
    ppermute x3, waiting for transfers between devices, passed_along(): return lax.ppermute(value, axis, pairs)  21.5 us
    ppermute x3, starting transfers between devices, passed_along(): return lax.ppermute(value, axis, pairs)  11.2 us
  transfers between devices with their start and end apart: 8, of which 8 were waited for; matrix products, arithmetic and copies ran while one was open for 10% of the time, Pallas kernels for 0%

commit v1 on v0

v1 whole, which is shorter than its diff:
```python
import functools

import jax
import jax.numpy as jnp
from jax import lax
from jax.experimental import pallas as pl
from jax.experimental.pallas import tpu as pltpu
from jax.sharding import PartitionSpec as P

HD = 128
BLK = 128
GEN_BLK = 2
CAP_BLK = 4
NT = 4
NL = 8
NF = 128
CHIP = 80
PART = 40
LINE = NL * CHIP
SLICE = 1280
HEADS = 5
SW = 384
MESH = pl.DeviceIdType.MESH
F32 = jnp.float32
BF16 = jnp.bfloat16

epsilon = 1e-06


def kernel(
    hid, cot, gain, wq, wk, wv, src, seg, pos,
    att, grad,
    W, V, X, N, stage, sib, tab_out, tab_in, qkv, probs, allow, vc,
    R, Rb, SR, H, P1, F, P2,
    sib_s, sib_r, tab_s, tab_r, xs, xr, xfs, xfr,
    p1s, p1r, v1s, v1r, rs, rr, vs, vr, fs, fr, gs, gr,
    ss, sr, q1s, q1r, q2s, q2r,
):
    g = lax.axis_index("fsdp")
    t = lax.axis_index("tp")
    c = g % 2
    y = (g // 2) % NL
    z = g // (2 * NL)
    a = y + c * (z - y)
    b = z + c * (y - z)

    def first(i):
        return ((z + c * (i - z)) * NL + (i + c * (y - i))) * 2 + c

    def second(i):
        return ((i + c * (z - i)) * NL + (y + c * (i - y))) * 2 + c

    sibling = g + 1 - 2 * c
    before = (g + NF - 1) % NF
    other = (g + NF - 1 + 2 * c) % NF
    right, left, across = (t + 1) % NT, (t + NT - 1) % NT, (t + 2) % NT

    barrier = pltpu.get_barrier_semaphore()

    def greet(f, s):
        pl.semaphore_signal(barrier, inc=1, device_id=(f, s), device_id_type=MESH)

    greet(sibling, t)
    greet(other, t)
    greet(g, right)
    greet(g, left)
    for k in range(1, NL):
        greet(first((a + k) % NL), t)
        greet(second((b + k) % NL), t)

    def remote(source, target, send, recv, f, s):
        return pltpu.make_async_remote_copy(
            src_ref=source, dst_ref=target, send_sem=send, recv_sem=recv,
            device_id=(f, s), device_id_type=MESH,
        )

    stream0 = jnp.concatenate([wq[:, : 2 * HD].astype(F32), wk[...].astype(F32)], axis=1)
    stream1 = wq[:, 2 * HD :].astype(F32)
    value_rows = wv[...].astype(F32)
    stage[:, :SW] = jnp.where(c == 0, stream1, stream0)
    stage[:, SW:] = value_rows

    def held(block):
        flag = jnp.int32(0)
        segment = jnp.int32(0)
        place = jnp.int32(0)
        for s in range(CAP_BLK):
            hit = src[s] == block
            flag = flag + jnp.where(hit, 1, 0)
            segment = segment + jnp.where(hit, seg[s], 0)
            place = place + jnp.where(hit, pos[s], 0)
        return flag, segment, place

    row = lax.broadcasted_iota(jnp.int32, (8, 128), 0)
    table = jnp.zeros((8, 128), jnp.int32)
    for block in range(GEN_BLK):
        for item, value in enumerate(held(GEN_BLK + block)):
            table = jnp.where(row == GEN_BLK * item + block, value, table)
    tab_out[...] = table

    pl.semaphore_wait(barrier, 4 + 2 * (NL - 1))

    sib_copy = remote(stage, sib, sib_s, sib_r, sibling, t)
    sib_copy.start()
    x_copies = []
    for d, h in ((0, 0), (1, 1), (0, 1), (1, 0)):
        copy = remote(
            hid.at[pl.ds(BLK * h, BLK)], X.at[t, h], xs.at[d, h], xr.at[d, h], g, (right, left)[d]
        )
        copy.start()
        x_copies.append(copy)
    tab_copy = remote(tab_out, tab_in, tab_s, tab_r, before, t)
    tab_copy.start()

    X[t, 0] = hid[:BLK, :]
    X[t, 1] = hid[BLK:, :]

    sib_copy.wait_recv()
    mine = jnp.where(c == 0, stream0, stream1)
    theirs = sib[:, :SW]
    top = jnp.where(c == 0, mine, theirs)
    bottom = jnp.where(c == 0, theirs, mine)
    W[c, z, y] = jnp.concatenate([top, bottom], axis=0).astype(BF16)
    top = jnp.where(c == 0, value_rows, sib[:, SW:])
    bottom = jnp.where(c == 0, sib[:, SW:], value_rows)

    @pl.when(c == 0)
    def _():
        V[z, y] = jnp.concatenate([top, bottom], axis=0).astype(BF16)

    p1 = []
    for k in (1, 7, 2, 6, 3, 5, 4):
        copy = remote(
            W.at[c, z, y], W.at[c, z, y], p1s.at[k], p1r.at[k], first((a + k) % NL), t
        )
        copy.start()
        p1.append(copy)
    v1 = []

    @pl.when(c == 0)
    def _():
        for k in (1, 7, 2, 6, 3, 5, 4):
            remote(
                V.at[z, y], V.at[z, y], v1s.at[k], v1r.at[k], first((a + k) % NL), t
            ).start()

    for copy in p1:
        copy.wait_recv()

    def piece(core, line, h):
        items = pl.ds(4 * h, 4)
        return W.at[0, line, items] if core == 0 else W.at[1, items, line]

    def each_core(body):
        for core in range(2):

            @pl.when(c == core)
            def _(core=core):
                body(core)

    def ring(core, d, s, h):
        line = (b + (NL - s, s)[d]) % NL
        ref = piece(core, line, h)
        target = second((b + (1, NL - 1)[d]) % NL)
        return remote(ref, ref, rs.at[d, s, h], rr.at[d, s, h], target, t)

    def arrival(core, d, s, h):
        line = (b + (NL - s, s)[d]) % NL
        ref = piece(core, line, h)
        target = second((b + (1, NL - 1)[d]) % NL)
        return remote(ref, ref, rs.at[d, s - 1, h], rr.at[d, s - 1, h], target, t)

    def to_sibling(core, d, s, h):
        line = (b + (NL - s, s)[d]) % NL
        ref = piece(core, line, h)
        return remote(ref, ref, fs.at[d, s, h], fr.at[d, s, h], sibling, t)

    def from_sibling(core, d, s, h):
        ref = piece(1 - core, (a + (NL - s, s)[d]) % NL, h)
        return remote(ref, ref, fs.at[d, s, h], fr.at[d, s, h], sibling, t)

    steps = [(0, 0, 0), (1, 0, 1), (0, 0, 1), (1, 0, 0)]
    for s in range(1, 4):
        steps += [(0, s, 0), (1, s, 1), (0, s, 1), (1, s, 0)]
    steps += [(0, 4, 0), (1, 4, 1)]
    sent = [p for p in steps if p[1] < 3 or (p[1] == 3 and p[0] == p[2])]
    shared = [p for p in steps if p[1] > 0 or p[0] == p[2]]

    def take(part):
        def body(core):
            if part[1] > 0:
                arrival(core, *part).wait_recv()
            if part in sent:
                ring(core, *part).start()
            if part in shared:
                to_sibling(core, *part).start()

        each_core(body)

    for part in steps[:4]:
        take(part)

    x_copies[0].wait_recv()
    fwd0 = remote(X.at[left, 0], X.at[left, 0], xfs.at[0], xfr.at[0], g, right)
    fwd0.start()
    x_copies[1].wait_recv()
    fwd1 = remote(X.at[right, 1], X.at[right, 1], xfs.at[1], xfr.at[1], g, left)
    fwd1.start()

    for part in steps[4:8]:
        take(part)

    def value_ring(d, s):
        line = (b + (NL - s, s)[d]) % NL
        return remote(
            V.at[line], V.at[line], vs.at[d, s], vr.at[d, s], second((b + (1, NL - 1)[d]) % NL), t
        )

    def value_arrival(d, s):
        line = (b + (NL - s, s)[d]) % NL
        return remote(
            V.at[line], V.at[line], vs.at[d, s - 1], vr.at[d, s - 1],
            second((b + (1, NL - 1)[d]) % NL), t,
        )

    def value_share(d, s):
        line = (z + (NL - s, s)[d]) % NL
        return remote(V.at[line], V.at[line], gs.at[d, s], gr.at[d, s], sibling, t)

    value_steps = [(0, 0), (1, 0), (0, 1), (1, 1), (0, 2), (1, 2), (0, 3), (1, 3), (0, 4)]
    value_sent = [p for p in value_steps if p[1] < (4, 3)[p[0]]]
    value_shared = [p for p in value_steps if p != (1, 0)]

    def take_value(part):
        @pl.when(c == 0)
        def _():
            if part[1] > 0:
                value_arrival(*part).wait_recv()
            if part in value_sent:
                value_ring(*part).start()
            if part in value_shared:
                value_share(*part).start()

    for part in steps[8:12]:
        take(part)

    @pl.when(c == 0)
    def _():
        for k in range(1, NL):
            remote(
                V.at[z, y], V.at[z, y], v1s.at[k], v1r.at[k], first((a + k) % NL), t
            ).wait_recv()

    take_value((0, 0))
    take_value((1, 0))

    x_copies[2].wait_recv()
    x_copies[3].wait_recv()
    fwd0.wait_recv()
    fwd1.wait_recv()
    for h in range(2):

        def norm_rows(i, carry, h=h):
            rows = pl.ds(pl.multiple_of(i * 16, 16), 16)
            total = jnp.zeros((16, 1), F32)
            for s in range(NT):
                wide = X[s, h, rows, :].astype(F32)
                total = total + jnp.sum(wide * wide, axis=1, keepdims=True)
            scale = lax.rsqrt(total / (NT * SLICE) + epsilon)
            out_rows = pl.ds(pl.multiple_of(h * BLK + i * 16, 16), 16)
            for s in range(NT):
                wide = X[s, h, rows, :].astype(F32)
                part = gain[:, s * SLICE : (s + 1) * SLICE]
                N[out_rows, s * SLICE : (s + 1) * SLICE] = (wide * scale * part).astype(BF16)
            return carry

        lax.fori_loop(0, BLK // 16, norm_rows, 0)

    for part in steps[12:]:
        take(part)

    take_value((0, 1))
    take_value((1, 1))

    for part in shared:
        each_core(lambda core, part=part: from_sibling(core, *part).wait_recv())

    for stream in range(2):

        def project(i, carry, stream=stream):
            features = pl.ds(pl.multiple_of(i * 2 * LINE, 2 * LINE), 2 * LINE)
            piece_w = W[stream, pl.ds(2 * i, 2)].reshape(2 * LINE, SW)
            prod = jnp.dot(N[:, features], piece_w, preferred_element_type=F32)
            qkv[stream] = jnp.where(i == 0, prod, qkv[stream] + prod)
            return carry

        qkv[stream] = jnp.zeros((GEN_BLK * BLK, SW), F32)
        lax.fori_loop(0, NL // 2, project, 0)

    take_value((0, 2))
    take_value((1, 2))

    tab_copy.wait_recv()
    info = []
    for block in range(GEN_BLK):
        flag, segment, place = held(block)
        there = tab_in[block : block + 1, :]
        info.append((
            flag + there,
            there,
            segment + tab_in[GEN_BLK + block : GEN_BLK + block + 1, :],
            place + tab_in[2 * GEN_BLK + block : 2 * GEN_BLK + block + 1, :],
        ))
    q_in = lax.broadcasted_iota(jnp.int32, (BLK, BLK), 0)
    k_in = lax.broadcasted_iota(jnp.int32, (BLK, BLK), 1)
    for i in range(GEN_BLK):
        for j in range(GEN_BLK):
            fi, li, si, pi = info[i]
            fj, lj, sj, pj = info[j]
            both = (fi > 0) & (fj > 0) & (li == lj) & (si == sj)
            meet = jnp.broadcast_to(jnp.where(both, 1, 0), (BLK, BLK))
            ordered = (pi * BLK + q_in) >= (pj * BLK + k_in)
            allow[i * BLK : (i + 1) * BLK, j * BLK : (j + 1) * BLK] = jnp.where(ordered, meet, 0)

    keys = qkv[0, :, 2 * HD :].astype(BF16)
    may = allow[...] > 0
    total = jnp.zeros((GEN_BLK * BLK, HD), F32)
    for head in range(HEADS):
        stream, at = (0, head) if head < 2 else (1, head - 2)
        queries = qkv[stream, :, at * HD : (at + 1) * HD].astype(BF16)
        scores = lax.dot_general(
            queries, keys, (((1,), (1,)), ((), ())), preferred_element_type=F32
        ) * HD ** (-0.5)
        masked = jnp.where(may, scores, -1e30)
        row_max = jnp.max(masked, axis=1, keepdims=True)
        raised = jnp.where(may, jnp.exp(masked - row_max), 0.0)
        denom = jnp.sum(raised, axis=1, keepdims=True)
        denom = jnp.where(denom == 0.0, 1.0, denom)
        prob = (raised / denom).astype(BF16)
        probs[head] = prob
        total = total + lax.dot_general(
            prob, cot[:, head * HD : (head + 1) * HD], (((0,), (0,)), ((), ())),
            preferred_element_type=F32,
        )
    vc[...] = total.astype(BF16)

    take_value((0, 3))
    take_value((1, 3))

    def terms(i, carry):
        features = pl.ds(pl.multiple_of(i * LINE, LINE), LINE)
        prod = lax.dot_general(
            N[:, features], vc[...], (((0,), (0,)), ((), ())), preferred_element_type=F32
        ).reshape(NL, CHIP, HD)
        R[0, :, pl.ds(pl.multiple_of(i * PART, PART), PART), :] = prod[:, :PART, :]
        R[1, i] = prod[:, PART:, :].reshape(NL * PART, HD)
        return carry

    lax.fori_loop(0, NL, terms, 0)
    Rb[...] = R[1 - c].astype(BF16)
    sum_copy = remote(Rb, SR, ss, sr, sibling, t)
    sum_copy.start()
    take_value((0, 4))
    sum_copy.wait_recv()
    for line in range(NL):
        both_cores = R[c, line] + SR[line].astype(F32)
        R[c, line] = both_cores
        H[line] = both_cores.astype(BF16)
    sums = []
    for k in (4, 3, 5, 2, 6, 1, 7):
        copy = remote(H.at[(a + k) % NL], P1.at[k], q1s.at[k], q1r.at[k], first((a + k) % NL), t)
        copy.start()
        sums.append(copy)

    @pl.when(c == 1)
    def _():
        for part in value_shared:
            value_share(*part).wait_recv()

    values = jnp.zeros((GEN_BLK * BLK, HD), F32)
    for i in range(NL):
        values = values + jnp.dot(
            N[:, i * LINE : (i + 1) * LINE], V[i].reshape(LINE, HD), preferred_element_type=F32
        )
    values = values.astype(BF16)
    for head in range(HEADS):
        att[:, head * HD : (head + 1) * HD] = jnp.dot(
            probs[head], values, preferred_element_type=F32
        ).astype(BF16)

    for copy in sums:
        copy.wait_recv()
    acc = R[c, a]
    for k in range(1, NL):
        acc = acc + P1[k].astype(F32)
    F[...] = acc.reshape(NL, PART, HD)
    last = []
    for k in (4, 3, 5, 2, 6, 1, 7):
        copy = remote(F.at[(b + k) % NL], P2.at[k], q2s.at[k], q2r.at[k], second((b + k) % NL), t)
        copy.start()
        last.append(copy)
    for copy in last:
        copy.wait_recv()
    out = F[b]
    for k in range(1, NL):
        out = out + P2[k]
    grad[...] = out

    sib_copy.wait_send()
    tab_copy.wait_send()
    fwd0.wait_send()
    fwd1.wait_send()
    sum_copy.wait_send()
    for copy in x_copies + p1 + sums + last:
        copy.wait_send()

    def all_left(core):
        for part in sent:
            ring(core, *part).wait_send()
        for part in shared:
            to_sibling(core, *part).wait_send()
        if core == 0:
            for k in range(1, NL):
                remote(
                    V.at[z, y], V.at[z, y], v1s.at[k], v1r.at[k], first((a + k) % NL), t
                ).wait_send()
            for part in value_sent:
                value_ring(*part).wait_send()
            for part in value_shared:
                value_share(*part).wait_send()

    each_core(all_left)


def shards(hidden_rows, cotangent, norm_gain, query_weight, key_weight, value_weight, source, segment, position):
    rows = GEN_BLK * BLK
    vmem = pl.BlockSpec(memory_space=pltpu.VMEM)
    smem = pl.BlockSpec(memory_space=pltpu.SMEM)
    dma = pltpu.SemaphoreType.DMA
    return pl.pallas_call(
        kernel,
        out_shape=(
            jax.ShapeDtypeStruct((rows, HEADS * HD), BF16),
            jax.ShapeDtypeStruct((PART, HD), F32),
        ),
        in_specs=[vmem] * 6 + [smem] * 3,
        out_specs=(vmem, vmem),
        scratch_shapes=[
            pltpu.VMEM((2, NL, NL, CHIP, SW), BF16),
            pltpu.VMEM((NL, NL, CHIP, HD), BF16),
            pltpu.VMEM((NT, GEN_BLK, BLK, SLICE), BF16),
            pltpu.VMEM((rows, NT * SLICE), BF16),
            pltpu.VMEM((PART, SW + HD), F32),
            pltpu.VMEM((PART, SW + HD), F32),
            pltpu.VMEM((8, 128), jnp.int32),
            pltpu.VMEM((8, 128), jnp.int32),
            pltpu.VMEM((2, rows, SW), F32),
            pltpu.VMEM((HEADS, rows, rows), BF16),
            pltpu.VMEM((rows, rows), jnp.int32),
            pltpu.VMEM((rows, HD), BF16),
            pltpu.VMEM((2, NL, NL * PART, HD), F32),
            pltpu.VMEM((NL, NL * PART, HD), BF16),
            pltpu.VMEM((NL, NL * PART, HD), BF16),
            pltpu.VMEM((NL, NL * PART, HD), BF16),
            pltpu.VMEM((NL, NL * PART, HD), BF16),
            pltpu.VMEM((NL, PART, HD), F32),
            pltpu.VMEM((NL, PART, HD), F32),
            dma, dma, dma, dma,
            dma((2, 2)), dma((2, 2)), dma((2,)), dma((2,)),
            dma((NL,)), dma((NL,)), dma((NL,)), dma((NL,)),
            dma((2, 4, 2)), dma((2, 4, 2)),
            dma((2, 4)), dma((2, 4)),
            dma((2, 5, 2)), dma((2, 5, 2)),
            dma((2, 5)), dma((2, 5)),
            dma, dma,
            dma((NL,)), dma((NL,)), dma((NL,)), dma((NL,)),
        ],
        compiler_params=pltpu.CompilerParams(
            collective_id=0, has_side_effects=True, vmem_limit_bytes=48 * 1024 * 1024
        ),
    )(
        hidden_rows, cotangent, norm_gain.reshape(1, -1), query_weight, key_weight, value_weight,
        source, segment, position,
    )


def solution(mesh):
    return jax.shard_map(
        shards,
        mesh=mesh,
        in_specs=(
            P("fsdp", "tp"),
            P("fsdp", "tp"),
            P(),
            P("fsdp", "tp"),
            P("fsdp", "tp"),
            P("fsdp", "tp"),
            P("fsdp"),
            P("fsdp"),
            P("fsdp"),
        ),
        out_specs=(P("fsdp", "tp"), P("fsdp", "tp")),
        check_vma=False,
    )
```

time: 549 us -> 87.7 us (0.16)
  waiting for transfers between devices: 461 us -> 0 us
  Pallas kernels: 0 us -> 79.6 us
  matrix products: 30.7 us -> 0 us
  other arithmetic: 21.6 us -> 0 us
  between operations: 14 us -> 0.67 us
  starting transfers between devices: 11.4 us -> 0 us
    all_gather x4 -> x0, waiting for transfers between devices: 264 us -> none  [the longest x1 82.5 us: shards(): lax.all_gather(query_weight, 'fsdp', axis=0, tiled=True)]
    unnamed x6 -> x0, waiting for transfers between devices: 176 us -> none
    pallas_call x0 -> x1, Pallas kernels: none -> 79.6 us  [shards(): pl.pallas_call(kernel, out_shape=(jax.ShapeDtypeStruct((rows, HEADS * HD)...]
    dot_general x4 -> x0, matrix products: 30.7 us -> none  [the longest x1 8.69 us: shards(): jnp.einsum('qgd,kd->gqk', queries, keys, preferred_element_type=jnp.float32)]
    ppermute x3 -> x0, waiting for transfers between devices: 21.5 us -> none  [passed_along(): return lax.ppermute(value, axis, pairs)]
    ppermute x3 -> x0, starting transfers between devices: 11.2 us -> none  [passed_along(): return lax.ppermute(value, axis, pairs)]
    sub x2 -> x0, other arithmetic: 6.95 us -> none  [the longest x1 6.88 us: shards(): raised = jnp.where(allow[None], jnp.exp(masked - row_max), 0.0)]
    unnamed x12 -> x20, local copies, waits for them, and re-layouts: 0.31 us -> 6.99 us
  transfers between devices with their start and end apart: 8 -> 0, of which waited for: 8 -> 0; matrix products, arithmetic and copies ran while one was open for 10% -> 0% of each run, Pallas kernels for 0% -> 0%
where the time goes in v1:
time: 87.7 us; the launch traced here: 87.3 us
  Pallas kernels  79.6 us (91%)
  local copies, waits for them, and re-layouts  6.99 us (8%)
    pallas_call x1, Pallas kernels, shards(): pl.pallas_call(kernel, out_shape=(jax.ShapeDtypeStruct((rows, HEADS * HD)...  79.6 us
    unnamed x20, local copies, waits for them, and re-layouts  6.99 us

profile of v1, /device:TPU:1, one launch (start us, length us, event | category | flops | bytes accessed | tf_op | source)
XLA Modules:
  0.0 87.3 jit_solution(18165490577993095456)
XLA Ops:
  0.6 0.0 copy-start.8
  0.6 0.0 copy-start.7
  0.7 0.0 copy-start.6
  0.7 0.6 copy-done.8
  1.3 0.0 copy-done.7
  1.3 0.0 copy-done.6
  1.3 0.0 copy-start
  1.3 1.1 %copy-done = bf16[256,1280]{1,0:T(8,128)(2,1)S(1)} copy-done((bf16[256,1280]{1,0:T(8,128)(2,1)S(1)}, bf16[256,1280]{1,0:T(8,128)(2,1)}, u32[]{:S(2)}) %copy-start) | copy-done | bytes 655384
  2.4 0.0 copy-start.1
  2.4 1.0 %copy-done.1 = bf16[256,640]{1,0:T(8,128)(2,1)S(1)} copy-done((bf16[256,640]{1,0:T(8,128)(2,1)S(1)}, bf16[256,640]{1,0:T(8,128)(2,1)}, u32[]{:S(2)}) %copy-start.1) | copy-done | bytes 327704
  3.4 0.0 copy-start.2
  3.4 0.8 copy-done.2
  4.2 0.0 copy-start.3
  4.2 0.7 copy-done.3
  4.9 0.0 copy-start.4
  4.9 0.7 copy-done.4
  5.6 0.0 copy-start.5
  5.6 0.7 copy-done.5
  6.3 79.6 %shard_map.104 = (bf16[256,640]{1,0:T(8,128)(2,1)S(1)}, f32[40,128]{1,0:T(8,128)S(1)}) custom-call(bf16[256,1280]{1,0:T(8,128)(2,1)S(1)} %copy-done, bf16[256,640]{1,0:T(8,128)(2,1)S(1)} %copy-done.1, f32[1,5120]{1,0:T(1,128)S(1)} %bitcast.1, bf16[40,640]{1,0:T(8,128)(2,1)S(1)} %copy-done.2, bf16[40,128]{1,0:T(8,128)(2,1)S(1)} %copy-done.4, ...), custom_call_target="tpu_custom_call" | custom-call | tf_op jit(solution)/shard_map/pallas_call | solution.py:440
  86.0 0.7 copy.13
  86.7 0.6 copy.14
Async XLA Ops:
  0.6 0.7 copy-start.8
  0.6 0.7 copy-start.7
  0.7 0.7 copy-start.6
  1.3 1.1 %copy-start = (bf16[256,1280]{1,0:T(8,128)(2,1)S(1)}, bf16[256,1280]{1,0:T(8,128)(2,1)}, u32[]{:S(2)}) copy-start(bf16[256,1280]{1,0:T(8,128)(2,1)} %hid.1) | copy-start | bytes 1966084
  2.4 1.0 %copy-start.1 = (bf16[256,640]{1,0:T(8,128)(2,1)S(1)}, bf16[256,640]{1,0:T(8,128)(2,1)}, u32[]{:S(2)}) copy-start(bf16[256,640]{1,0:T(8,128)(2,1)} %cot.1) | copy-start | bytes 983044
  3.4 0.8 copy-start.2
  4.2 0.7 copy-start.3
  4.9 0.7 copy-start.4
  5.6 0.7 copy-start.5

commit v2 on v1

v2 whole, which is shorter than its diff:
```python
import functools

import jax
import jax.numpy as jnp
from jax import lax
from jax.experimental import pallas as pl
from jax.experimental.pallas import tpu as pltpu
from jax.sharding import PartitionSpec as P

HD = 128
BLK = 128
GEN_BLK = 2
CAP_BLK = 4
NT_X = 4
NL = 8
NF = 128
CHIP = 80
PART = 40
LINE = NL * CHIP
SLICE = 1280
HEADS = 5
SW = 384
MESH = pl.DeviceIdType.MESH
F32 = jnp.float32
BF16 = jnp.bfloat16

epsilon = 1e-06


def kernel(
    hid, cot_in, gain_in, wq_in, wk_in, wv_in, src_in, seg_in, pos_in,
    att, grad,
    cot, gain, wq, wk, wv, src, seg, pos,
    W, V, X, NT, stage, sib, tab_out, tab_in, qkv, probs, allow, vc, sq_out, sq_in, scale,
    R, Rb, SR, H, M, P1, F, P2,
    ld, sib_s, sib_r, tab_s, tab_r, xs, xr, xfs, xfr,
    sqs, sqr, p1s, p1r, v1s, v1r, os, rs, rr, vs, vr, fs, fr, f4s, f4r, gs, gr,
    ss, sr, ms, mr, q1s, q1r, q2s, q2r,
):
    g = lax.axis_index("fsdp")
    t = lax.axis_index("tp")
    c = g % 2
    y = (g // 2) % NL
    z = g // (2 * NL)
    a = y + c * (z - y)
    b = z + c * (y - z)

    def first(i):
        return ((z + c * (i - z)) * NL + (i + c * (y - i))) * 2 + c

    def second(i):
        return ((i + c * (z - i)) * NL + (y + c * (i - y))) * 2 + c

    sibling = g + 1 - 2 * c
    before = (g + NF - 1) % NF
    other = (g + NF - 1 + 2 * c) % NF
    right, left, across = (t + 1) % NT_X, (t + NT_X - 1) % NT_X, (t + 2) % NT_X

    barrier = pltpu.get_barrier_semaphore()

    def greet(f, s):
        pl.semaphore_signal(barrier, inc=1, device_id=(f, s), device_id_type=MESH)

    greet(sibling, t)
    greet(other, t)
    for s in (right, left, across):
        greet(g, s)
    for k in (1, 2, NL - 2, NL - 1):
        greet(first((a + k) % NL), t)
    for k in (1, NL - 1):
        greet(second((b + k) % NL), t)

    def remote(source, target, send, recv, f, s):
        return pltpu.make_async_remote_copy(
            src_ref=source, dst_ref=target, send_sem=send, recv_sem=recv,
            device_id=(f, s), device_id_type=MESH,
        )

    loads = {}
    for i, (name, source, target) in enumerate((
        ("wq", wq_in, wq), ("wk", wk_in, wk), ("wv", wv_in, wv),
        ("src", src_in, src), ("seg", seg_in, seg), ("pos", pos_in, pos),
        ("gain", gain_in, gain),
        ("x0", hid.at[pl.ds(0, BLK)], X.at[t, 0]), ("x1", hid.at[pl.ds(BLK, BLK)], X.at[t, 1]),
        ("cot", cot_in, cot),
    )):
        loads[name] = pltpu.make_async_copy(source, target, ld.at[i])
        loads[name].start()

    for name in ("wq", "wk", "wv"):
        loads[name].wait()
    stream0 = jnp.concatenate([wq[:, : 2 * HD].astype(F32), wk[...].astype(F32)], axis=1)
    stream1 = wq[:, 2 * HD :].astype(F32)
    value_rows = wv[...].astype(F32)
    stage[:, :SW] = jnp.where(c == 0, stream1, stream0)
    stage[:, SW:] = value_rows

    for name in ("src", "seg", "pos"):
        loads[name].wait()

    def held(block):
        flag = jnp.int32(0)
        segment = jnp.int32(0)
        place = jnp.int32(0)
        for s in range(CAP_BLK):
            hit = src[s] == block
            flag = flag + jnp.where(hit, 1, 0)
            segment = segment + jnp.where(hit, seg[s], 0)
            place = place + jnp.where(hit, pos[s], 0)
        return flag, segment, place

    row = lax.broadcasted_iota(jnp.int32, (8, 128), 0)
    table = jnp.zeros((8, 128), jnp.int32)
    for block in range(GEN_BLK):
        for item, value in enumerate(held(GEN_BLK + block)):
            table = jnp.where(row == GEN_BLK * item + block, value, table)
    tab_out[...] = table

    for name in ("x0", "x1"):
        loads[name].wait()
    squares = jnp.zeros((GEN_BLK * BLK, 128), F32)
    for j in range(SLICE // 128):
        wide = X[t, :, :, j * 128 : (j + 1) * 128].reshape(GEN_BLK * BLK, 128).astype(F32)
        squares = squares + wide * wide
    own_squares = jnp.sum(squares.T, axis=0, keepdims=True)
    sq_out[...] = jnp.broadcast_to(own_squares, (8, GEN_BLK * BLK))

    pl.semaphore_wait(barrier, 11)

    sib_copy = remote(stage, sib, sib_s, sib_r, sibling, t)
    sib_copy.start()
    sq_copies = [
        remote(sq_out, sq_in.at[i], sqs.at[i], sqr.at[i], g, s)
        for i, s in enumerate((right, left, across))
    ]
    for copy in sq_copies:
        copy.start()
    x_copies = []
    for d, h in ((0, 0), (1, 1), (0, 1), (1, 0)):
        copy = remote(
            hid.at[pl.ds(BLK * h, BLK)], X.at[t, h], xs.at[d, h], xr.at[d, h], g, (right, left)[d]
        )
        copy.start()
        x_copies.append(copy)
    tab_copy = remote(tab_out, tab_in, tab_s, tab_r, before, t)
    tab_copy.start()

    sib_copy.wait_recv()
    mine = jnp.where(c == 0, stream0, stream1)
    theirs = sib[:, :SW]
    top = jnp.where(c == 0, mine, theirs)
    bottom = jnp.where(c == 0, theirs, mine)
    W[c, z, y] = jnp.concatenate([top, bottom], axis=0).astype(BF16)

    def each_core(body):
        for core in range(2):

            @pl.when(c == core)
            def _(core=core):
                body(core)

    def block_ref(item):
        return W.at[c, z + c * (item - z), item + c * (y - item)]

    def along(i):
        whose, to = ((0, 1), (0, 7), (0, 2), (0, 6), (7, 2), (1, 6), (6, 2))[i]
        ref = block_ref((a + whose) % NL)
        return remote(ref, ref, p1s.at[i], p1r.at[i], first((a + to) % NL), t)

    got = (7, 1, 6, 2, 5, 3, 4)

    def along_arrival(i):
        ref = block_ref((a + got[i]) % NL)
        return remote(ref, ref, p1s.at[i], p1r.at[i], first((a + got[i]) % NL), t)

    def own_line(k, d):
        item = (a + k) % NL
        ref = block_ref(item)
        return remote(
            ref, ref, os.at[d, k], rr.at[d, 0, (item // 2 + 4 - a // 2) % 4],
            second((b + (1, NL - 1)[d]) % NL), t,
        )

    def take_block(i):
        along_arrival(i).wait_recv()
        if i < 3:
            along(4 + i).start()
        own_line(got[i], 0).start()
        own_line(got[i], 1).start()

    for i in range(4):
        along(i).start()
    own_line(0, 0).start()
    own_line(0, 1).start()
    for i in range(4):
        take_block(i)

    def piece(core, line, j):
        items = pl.ds(2 * ((a // 2 + j) % 4), 2)
        return W.at[0, line, items] if core == 0 else W.at[1, items, line]

    def whole(core, line):
        return W.at[0, line] if core == 0 else W.at[1, :, line]

    def ring(core, d, s, j):
        ref = piece(core, (b + (NL - s, s)[d]) % NL, j)
        target = second((b + (1, NL - 1)[d]) % NL)
        return remote(ref, ref, rs.at[d, s, j], rr.at[d, s, j], target, t)

    def arrival(core, d, s, j):
        ref = piece(core, (b + (NL - s, s)[d]) % NL, j)
        target = second((b + (1, NL - 1)[d]) % NL)
        return remote(ref, ref, rs.at[d, s - 1, j], rr.at[d, s - 1, j], target, t)

    def to_sibling(core, d, s):
        ref = whole(core, (b + (NL - s, s)[d]) % NL)
        return remote(ref, ref, fs.at[d, s], fr.at[d, s], sibling, t)

    def from_sibling(core, d, s):
        ref = whole(1 - core, (a + (NL - s, s)[d]) % NL)
        return remote(ref, ref, fs.at[d, s], fr.at[d, s], sibling, t)

    def last_to_sibling(core, j):
        ref = piece(core, (b + 4) % NL, j)
        return remote(ref, ref, f4s.at[j], f4r.at[j], sibling, t)

    def last_from_sibling(core, j):
        items = pl.ds(2 * ((b // 2 + j) % 4), 2)
        line = (a + 4) % NL
        ref = W.at[0, line, items] if core == 1 else W.at[1, items, line]
        return remote(ref, ref, f4s.at[j], f4r.at[j], sibling, t)

    order = (0, 1, 3, 2)
    steps = [(d, s, j) for s in range(1, 4) for j in order for d in range(2)]
    last_steps = [(0, 4, 0), (1, 4, 3), (0, 4, 1), (1, 4, 2)]
    sent = [p for p in steps if p[1] < 3 or p[2] in ((0, 1), (3, 2))[p[0]]]

    def take(s, js):
        def body(core):
            for part in steps + last_steps:
                if part[1] == s and part[2] in js:
                    arrival(core, *part).wait_recv()
                    if part in sent:
                        ring(core, *part).start()
                    if s == 4:
                        last_to_sibling(core, part[2]).start()

        each_core(body)

    def share(s):
        each_core(lambda core: [to_sibling(core, d, s).start() for d in range(min(s + 1, 2))])

    def from_other(s):
        def body(core):
            if s == 4:
                for j in order:
                    last_from_sibling(core, j).wait_recv()
            else:
                for d in range(min(s + 1, 2)):
                    from_sibling(core, d, s).wait_recv()

        each_core(body)

    take(1, (0,))
    for i in range(4, 7):
        take_block(i)
    share(0)

    top = jnp.where(c == 0, value_rows, sib[:, SW:])
    bottom = jnp.where(c == 0, sib[:, SW:], value_rows)

    def value_first(k):
        return remote(
            V.at[z, y], V.at[z, y], v1s.at[k], v1r.at[k], first((a + k) % NL), t
        )

    @pl.when(c == 0)
    def _():
        V[z, y] = jnp.concatenate([top, bottom], axis=0).astype(BF16)
        for k in (1, 7, 2, 6, 3, 5, 4):
            value_first(k).start()

    x_copies[0].wait_recv()
    fwd0 = remote(X.at[left, 0], X.at[left, 0], xfs.at[0], xfr.at[0], g, right)
    fwd0.start()
    x_copies[1].wait_recv()
    fwd1 = remote(X.at[right, 1], X.at[right, 1], xfs.at[1], xfr.at[1], g, left)
    fwd1.start()

    total = own_squares
    for i, copy in enumerate(sq_copies):
        copy.wait_recv()
        total = total + sq_in[i, :1, :]
    by_token = lax.rsqrt(total / (NT_X * SLICE) + epsilon)
    scale[...] = jnp.broadcast_to(by_token, (128, GEN_BLK * BLK)).T

    def prepare(s):
        def half_slice(i, carry):
            blocks = []
            for j in range(5):
                columns = pl.ds(pl.multiple_of(i * LINE + j * 128, 128), 128)
                wide = X[s, :, :, columns].reshape(GEN_BLK * BLK, 128).astype(F32)
                blocks.append((wide * scale[...] * gain[s, :, columns]).astype(BF16).T)
            NT[2 * s + i] = jnp.concatenate(blocks, axis=0).reshape(NL, CHIP, GEN_BLK * BLK)
            return carry

        lax.fori_loop(0, 2, half_slice, 0)

    loads["gain"].wait()
    take(1, (1,))
    prepare(t)
    take(1, (3, 2))
    share(1)
    take(2, (0, 1, 3))
    x_copies[2].wait_recv()
    x_copies[3].wait_recv()
    prepare(left)
    take(2, (2,))
    share(2)
    prepare(right)
    take(3, (0, 1, 3, 2))
    share(3)

    def value_ring(d, s):
        line = (b + (NL - s, s)[d]) % NL
        return remote(
            V.at[line], V.at[line], vs.at[d, s], vr.at[d, s], second((b + (1, NL - 1)[d]) % NL), t
        )

    def value_arrival(d, s):
        line = (b + (NL - s, s)[d]) % NL
        return remote(
            V.at[line], V.at[line], vs.at[d, s - 1], vr.at[d, s - 1],
            second((b + (1, NL - 1)[d]) % NL), t,
        )

    def value_share(d, s):
        line = (z + (NL - s, s)[d]) % NL
        return remote(V.at[line], V.at[line], gs.at[d, s], gr.at[d, s], sibling, t)

    value_steps = [(0, 0), (1, 0), (0, 1), (1, 1), (0, 2), (1, 2), (0, 3), (1, 3), (0, 4)]
    value_sent = [p for p in value_steps if p[1] < (4, 3)[p[0]]]
    value_shared = [p for p in value_steps if p != (1, 0)]

    def take_value(s):
        @pl.when(c == 0)
        def _():
            for part in value_steps:
                if part[1] == s:
                    if s > 0:
                        value_arrival(*part).wait_recv()
                    if part in value_sent:
                        value_ring(*part).start()
                    if part in value_shared:
                        value_share(*part).start()

    @pl.when(c == 0)
    def _():
        for k in range(1, NL):
            value_first(k).wait_recv()

    take_value(0)
    fwd0.wait_recv()
    fwd1.wait_recv()
    prepare(across)

    def project(one, two, fresh):
        for stream in range(2):
            def pick(ref, line, stream=stream):
                return ref[line] if stream == 0 else ref[:, line]

            at = (z, y)[stream]
            l0, l1 = (at + one) % NL, (at + two) % NL
            rows = jnp.concatenate(
                [pick(NT, l0).reshape(LINE, -1), pick(NT, l1).reshape(LINE, -1)], axis=0
            )
            weights = jnp.concatenate(
                [pick(W.at[stream], l0).reshape(LINE, -1), pick(W.at[stream], l1).reshape(LINE, -1)],
                axis=0,
            )
            prod = lax.dot_general(
                rows, weights, (((0,), (0,)), ((), ())), preferred_element_type=F32
            )
            qkv[stream] = prod if fresh else qkv[stream] + prod

    from_other(0)
    from_other(1)
    project(1, 7, True)
    from_other(2)
    project(2, 6, False)
    take(4, order)
    from_other(3)
    project(3, 5, False)

    tab_copy.wait_recv()
    info = []
    for block in range(GEN_BLK):
        flag, segment, place = held(block)
        there = tab_in[block : block + 1, :]
        info.append((
            flag + there,
            there,
            segment + tab_in[GEN_BLK + block : GEN_BLK + block + 1, :],
            place + tab_in[2 * GEN_BLK + block : 2 * GEN_BLK + block + 1, :],
        ))
    q_in = lax.broadcasted_iota(jnp.int32, (BLK, BLK), 0)
    k_in = lax.broadcasted_iota(jnp.int32, (BLK, BLK), 1)
    for i in range(GEN_BLK):
        for j in range(GEN_BLK):
            fi, li, si, pi = info[i]
            fj, lj, sj, pj = info[j]
            both = (fi > 0) & (fj > 0) & (li == lj) & (si == sj)
            meet = jnp.broadcast_to(jnp.where(both, 1, 0), (BLK, BLK))
            ordered = (pi * BLK + q_in) >= (pj * BLK + k_in)
            allow[i * BLK : (i + 1) * BLK, j * BLK : (j + 1) * BLK] = jnp.where(ordered, meet, 0)

    take_value(1)
    from_other(4)
    project(0, 4, False)

    loads["cot"].wait()
    keys = qkv[0, :, 2 * HD :].astype(BF16)
    may = allow[...] > 0
    total = jnp.zeros((GEN_BLK * BLK, HD), F32)
    for head in range(HEADS):
        stream, at = (0, head) if head < 2 else (1, head - 2)
        queries = qkv[stream, :, at * HD : (at + 1) * HD].astype(BF16)
        scores = lax.dot_general(
            queries, keys, (((1,), (1,)), ((), ())), preferred_element_type=F32
        ) * HD ** (-0.5)
        masked = jnp.where(may, scores, -1e30)
        row_max = jnp.max(masked, axis=1, keepdims=True)
        raised = jnp.where(may, jnp.exp(masked - row_max), 0.0)
        denom = jnp.sum(raised, axis=1, keepdims=True)
        denom = jnp.where(denom == 0.0, 1.0, denom)
        prob = (raised / denom).astype(BF16)
        probs[head] = prob
        total = total + lax.dot_general(
            prob, cot[:, head * HD : (head + 1) * HD], (((0,), (0,)), ((), ())),
            preferred_element_type=F32,
        )
    vc[...] = total.astype(BF16)
    take_value(2)

    def sum_copy(i):
        return remote(Rb.at[i], SR.at[i], ss.at[i], sr.at[i], sibling, t)

    def terms(i, carry):
        rows = jnp.concatenate(
            [NT[i + c * (m - i), m + c * (i - m)] for m in range(NL)], axis=0
        )
        prod = jnp.dot(rows, vc[...], preferred_element_type=F32).reshape(NL, CHIP, HD)
        top, bottom = prod[:, :PART, :], prod[:, PART:, :]
        Rb[i] = jnp.where(c == 0, bottom, top).reshape(NL * PART, HD).astype(BF16)
        sum_copy(i).start()
        R[:, pl.ds(pl.multiple_of(i * PART, 8), PART), :] = jnp.where(c == 0, top, bottom)
        return carry

    lax.fori_loop(0, NL, terms, 0)

    def both_cores(k):
        line = (a + k) % NL
        sum_copy(line).wait_recv()
        return R[line] + SR[line].astype(F32)

    H[4] = both_cores(4).astype(BF16)
    merge = remote(H.at[4], M, ms, mr, first((a + NL - 1) % NL), t)
    merge.start()
    sums = []
    for k in (3, 2, 6, 5, 1, 7):
        value = both_cores(k)
        if k == 5:
            merge.wait_recv()
            value = value + M[...].astype(F32)
        H[k] = value.astype(BF16)
        copy = remote(H.at[k], P1.at[k], q1s.at[k], q1r.at[k], first((a + k) % NL), t)
        copy.start()
        sums.append(copy)
    acc = both_cores(0)

    take_value(3)
    for copy in sums:
        copy.wait_recv()
    for k in (1, 2, 3, 5, 6, 7):
        acc = acc + P1[k].astype(F32)
    F[...] = acc.reshape(NL, PART, HD)
    last = []
    for k in (4, 3, 5, 2, 6, 1, 7):
        copy = remote(F.at[(b + k) % NL], P2.at[k], q2s.at[k], q2r.at[k], second((b + k) % NL), t)
        copy.start()
        last.append(copy)
    take_value(4)

    @pl.when(c == 1)
    def _():
        for part in value_shared:
            value_share(*part).wait_recv()

    values = jnp.zeros((GEN_BLK * BLK, HD), F32)
    for i in range(NL):
        values = values + lax.dot_general(
            NT[i].reshape(LINE, -1), V[i].reshape(LINE, HD), (((0,), (0,)), ((), ())),
            preferred_element_type=F32,
        )
    values = values.astype(BF16)
    for head in range(HEADS):
        att[:, head * HD : (head + 1) * HD] = jnp.dot(
            probs[head], values, preferred_element_type=F32
        ).astype(BF16)

    for copy in last:
        copy.wait_recv()
    out = F[b]
    for k in range(1, NL):
        out = out + P2[k]
    grad[...] = out

    for copy in x_copies + sq_copies + sums + last + [sib_copy, tab_copy, fwd0, fwd1, merge]:
        copy.wait_send()
    for i in range(NL):
        sum_copy(i).wait_send()
    for i in range(7):
        along(i).wait_send()
    for k in range(NL):
        own_line(k, 0).wait_send()
        own_line(k, 1).wait_send()

    def all_left(core):
        for part in sent:
            ring(core, *part).wait_send()
        for s in range(4):
            for d in range(min(s + 1, 2)):
                to_sibling(core, d, s).wait_send()
        for j in order:
            last_to_sibling(core, j).wait_send()
        if core == 0:
            for k in range(1, NL):
                value_first(k).wait_send()
            for part in value_sent:
                value_ring(*part).wait_send()
            for part in value_shared:
                value_share(*part).wait_send()

    each_core(all_left)


def shards(hidden_rows, cotangent, norm_gain, query_weight, key_weight, value_weight, source, segment, position):
    rows = GEN_BLK * BLK
    vmem = pl.BlockSpec(memory_space=pltpu.VMEM)
    dma = pltpu.SemaphoreType.DMA
    return pl.pallas_call(
        kernel,
        out_shape=(
            jax.ShapeDtypeStruct((rows, HEADS * HD), BF16),
            jax.ShapeDtypeStruct((PART, HD), F32),
        ),
        in_specs=[pl.BlockSpec(memory_space=pltpu.HBM)] * 9,
        out_specs=(vmem, vmem),
        scratch_shapes=[
            pltpu.VMEM((rows, HEADS * HD), BF16),
            pltpu.VMEM((NT_X, 1, SLICE), F32),
            pltpu.VMEM((PART, HEADS * HD), BF16),
            pltpu.VMEM((PART, HD), BF16),
            pltpu.VMEM((PART, HD), BF16),
            pltpu.SMEM((CAP_BLK,), jnp.int32),
            pltpu.SMEM((CAP_BLK,), jnp.int32),
            pltpu.SMEM((CAP_BLK,), jnp.int32),
            pltpu.VMEM((2, NL, NL, CHIP, SW), BF16),
            pltpu.VMEM((NL, NL, CHIP, HD), BF16),
            pltpu.VMEM((NT_X, GEN_BLK, BLK, SLICE), BF16),
            pltpu.VMEM((NL, NL, CHIP, rows), BF16),
            pltpu.VMEM((PART, SW + HD), F32),
            pltpu.VMEM((PART, SW + HD), F32),
            pltpu.VMEM((8, 128), jnp.int32),
            pltpu.VMEM((8, 128), jnp.int32),
            pltpu.VMEM((2, rows, SW), F32),
            pltpu.VMEM((HEADS, rows, rows), BF16),
            pltpu.VMEM((rows, rows), jnp.int32),
            pltpu.VMEM((rows, HD), BF16),
            pltpu.VMEM((8, rows), F32),
            pltpu.VMEM((3, 8, rows), F32),
            pltpu.VMEM((rows, HD), F32),
            pltpu.VMEM((NL, NL * PART, HD), F32),
            pltpu.VMEM((NL, NL * PART, HD), BF16),
            pltpu.VMEM((NL, NL * PART, HD), BF16),
            pltpu.VMEM((NL, NL * PART, HD), BF16),
            pltpu.VMEM((NL * PART, HD), BF16),
            pltpu.VMEM((NL, NL * PART, HD), BF16),
            pltpu.VMEM((NL, PART, HD), F32),
            pltpu.VMEM((NL, PART, HD), F32),
            dma((10,)),
            dma, dma, dma, dma,
            dma((2, 2)), dma((2, 2)), dma((2,)), dma((2,)),
            dma((3,)), dma((3,)),
            dma((7,)), dma((7,)),
            dma((NL,)), dma((NL,)),
            dma((2, NL)),
            dma((2, 4, 4)), dma((2, 4, 4)),
            dma((2, 4)), dma((2, 4)),
            dma((2, 4)), dma((2, 4)), dma((4,)), dma((4,)),
            dma((2, 5)), dma((2, 5)),
            dma((NL,)), dma((NL,)),
            dma, dma,
            dma((NL,)), dma((NL,)), dma((NL,)), dma((NL,)),
        ],
        compiler_params=pltpu.CompilerParams(
            collective_id=0, has_side_effects=True, vmem_limit_bytes=60 * 1024 * 1024
        ),
    )(
        hidden_rows, cotangent, norm_gain.reshape(NT_X, 1, SLICE), query_weight, key_weight, value_weight,
        source, segment, position,
    )


def solution(mesh):
    return jax.shard_map(
        shards,
        mesh=mesh,
        in_specs=(
            P("fsdp", "tp"),
            P("fsdp", "tp"),
            P(),
            P("fsdp", "tp"),
            P("fsdp", "tp"),
            P("fsdp", "tp"),
            P("fsdp"),
            P("fsdp"),
            P("fsdp"),
        ),
        out_specs=(P("fsdp", "tp"), P("fsdp", "tp")),
        check_vma=False,
    )
```

time: 87.7 us -> 75.5 us (0.86)
  Pallas kernels: 79.6 us -> 71.7 us
  local copies, waits for them, and re-layouts: 6.99 us -> 2.34 us
    pallas_call x1, Pallas kernels: 79.6 us -> 71.7 us  [shards(): pl.pallas_call(kernel, out_shape=(jax.ShapeDtypeStruct((rows, HEADS * HD)...]
    unnamed x20 -> x4, local copies, waits for them, and re-layouts: 6.99 us -> 2.34 us
where the time goes in v2:
time: 75.5 us; the launch traced here: 74.7 us
  Pallas kernels  71.7 us (95%)
  local copies, waits for them, and re-layouts  2.34 us (3%)
    pallas_call x1, Pallas kernels, shards(): pl.pallas_call(kernel, out_shape=(jax.ShapeDtypeStruct((rows, HEADS * HD)...  71.7 us
    unnamed x4, local copies, waits for them, and re-layouts  2.34 us

profile of v2, /device:TPU:1, one launch (start us, length us, event | category | flops | bytes accessed | tf_op | source)
XLA Modules:
  0.0 74.7 jit_solution(5752902139548606954)
XLA Ops:
  0.6 71.7 %shard_map.104 = (bf16[256,640]{1,0:T(8,128)(2,1)}, f32[40,128]{1,0:T(8,128)}) custom-call(bf16[256,1280]{1,0:T(8,128)(2,1)} %hid.1, bf16[256,640]{1,0:T(8,128)(2,1)} %cot_in.1, f32[4,1,1280]{2,1,0:T(1,128)} %bitcast.1, bf16[40,640]{1,0:T(8,128)(2,1)} %wq_in.1, bf16[40,128]{1,0:T(8,128)(2,1)} %wk_in.1, bf16[40,128]{1,0:T(8,128)(2,1)} %wv_in.1, s32[4]{0:T(128)} %src_in.1, ...), custom_call_target="tpu_custom_call" | custom-call | tf_op jit(solution)/shard_map/pallas_call | solution.py:551
  72.3 0.0 copy-start
  72.3 1.7 %copy.13 = bf16[256,640]{1,0:T(8,128)(2,1)} copy(bf16[256,640]{1,0:T(8,128)(2,1)} %get-tuple-element.4) | data formatting | bytes 655360
  74.1 0.0 copy-done
  74.1 0.6 copy.14
Async XLA Ops:
  72.3 1.7 %copy-start = (f32[40,128]{1,0:T(8,128)S(1)}, f32[40,128]{1,0:T(8,128)}, u32[]{:S(2)}) copy-start(f32[40,128]{1,0:T(8,128)} %get-tuple-element.5) | copy-start | bytes 61444

commit v3 on v2

--- a/solution.py
+++ b/solution.py
@@ -32,10 +32,10 @@
     att, grad,
     cot, gain, wq, wk, wv, src, seg, pos,
     W, V, X, NT, stage, sib, tab_out, tab_in, qkv, probs, allow, vc, sq_out, sq_in, scale,
-    R, Rb, SR, H, M, P1, F, P2,
+    TH, TH_in, top_rows, vc_in, R, H, M, P1, F, P2,
     ld, sib_s, sib_r, tab_s, tab_r, xs, xr, xfs, xfr,
     sqs, sqr, p1s, p1r, v1s, v1r, os, rs, rr, vs, vr, fs, fr, f4s, f4r, gs, gr,
-    ss, sr, ms, mr, q1s, q1r, q2s, q2r,
+    ths, thr, vcs, vcr, ms, mr, q1s, q1r, q2s, q2r,
 ):
     g = lax.axis_index("fsdp")
     t = lax.axis_index("tp")
@@ -163,7 +163,7 @@
         return W.at[c, z + c * (item - z), item + c * (y - item)]
 
     def along(i):
-        whose, to = ((0, 1), (0, 7), (0, 2), (0, 6), (7, 2), (1, 6), (6, 2))[i]
+        whose, to = ((0, 1), (0, 7), (0, 2), (0, 6), (6, 1), (2, 7), (6, 2))[i]
         ref = block_ref((a + whose) % NL)
         return remote(ref, ref, p1s.at[i], p1r.at[i], first((a + to) % NL), t)
 
@@ -171,7 +171,7 @@
 
     def along_arrival(i):
         ref = block_ref((a + got[i]) % NL)
-        return remote(ref, ref, p1s.at[i], p1r.at[i], first((a + got[i]) % NL), t)
+        return remote(ref, ref, p1s.at[i], p1r.at[i], first((a + 1) % NL), t)
 
     def own_line(k, d):
         item = (a + k) % NL
@@ -183,8 +183,8 @@
 
     def take_block(i):
         along_arrival(i).wait_recv()
-        if i < 3:
-            along(4 + i).start()
+        for relay in ((), (), (4, 6), (5,), (), (), ())[i]:
+            along(relay).start()
         own_line(got[i], 0).start()
         own_line(got[i], 1).start()
 
@@ -230,15 +230,15 @@
         ref = W.at[0, line, items] if core == 1 else W.at[1, items, line]
         return remote(ref, ref, f4s.at[j], f4r.at[j], sibling, t)
 
-    order = (0, 1, 3, 2)
-    steps = [(d, s, j) for s in range(1, 4) for j in order for d in range(2)]
+    orders = ((0, 1, 3, 2), (0, 3, 2, 1))
+    steps = [(d, s, orders[d][i]) for s in range(1, 4) for i in range(4) for d in range(2)]
     last_steps = [(0, 4, 0), (1, 4, 3), (0, 4, 1), (1, 4, 2)]
     sent = [p for p in steps if p[1] < 3 or p[2] in ((0, 1), (3, 2))[p[0]]]
 
-    def take(s, js):
+    def take(s, places):
         def body(core):
             for part in steps + last_steps:
-                if part[1] == s and part[2] in js:
+                if part[1] == s and orders[part[0]].index(part[2]) in places:
                     arrival(core, *part).wait_recv()
                     if part in sent:
                         ring(core, *part).start()
@@ -253,7 +253,7 @@
     def from_other(s):
         def body(core):
             if s == 4:
-                for j in order:
+                for j in range(4):
                     last_from_sibling(core, j).wait_recv()
             else:
                 for d in range(min(s + 1, 2)):
@@ -274,7 +274,7 @@
             V.at[z, y], V.at[z, y], v1s.at[k], v1r.at[k], first((a + k) % NL), t
         )
 
-    @pl.when(c == 0)
+    @pl.when(c == 1)
     def _():
         V[z, y] = jnp.concatenate([top, bottom], axis=0).astype(BF16)
         for k in (1, 7, 2, 6, 3, 5, 4):
@@ -295,55 +295,46 @@
     scale[...] = jnp.broadcast_to(by_token, (128, GEN_BLK * BLK)).T
 
     def prepare(s):
-        def half_slice(i, carry):
+        for i in range(2):
             blocks = []
             for j in range(5):
-                columns = pl.ds(pl.multiple_of(i * LINE + j * 128, 128), 128)
+                columns = pl.ds(i * LINE + j * 128, 128)
                 wide = X[s, :, :, columns].reshape(GEN_BLK * BLK, 128).astype(F32)
-                blocks.append((wide * scale[...] * gain[s, :, columns]).astype(BF16).T)
-            NT[2 * s + i] = jnp.concatenate(blocks, axis=0).reshape(NL, CHIP, GEN_BLK * BLK)
-            return carry
-
-        lax.fori_loop(0, 2, half_slice, 0)
+                blocks.append((wide * scale[...] * gain[s, :, columns]).T)
+            line = jnp.concatenate(blocks, axis=0).reshape(NL, CHIP, GEN_BLK * BLK)
+            NT[2 * s + i] = line.astype(BF16)
+            TH[1, 2 * s + i] = line[:, PART:].reshape(NT_X, CHIP, -1).astype(BF16)
+            top_rows[:, i * PART : (i + 1) * PART, :] = line[:, :PART]
+        TH[0, :, s] = top_rows[...].astype(BF16)
 
     loads["gain"].wait()
     take(1, (1,))
     prepare(t)
-    take(1, (3, 2))
+    take(1, (2, 3))
     share(1)
-    take(2, (0, 1, 3))
-    x_copies[2].wait_recv()
-    x_copies[3].wait_recv()
-    prepare(left)
-    take(2, (2,))
-    share(2)
-    prepare(right)
-    take(3, (0, 1, 3, 2))
-    share(3)
+    def value_line(at, d, s):
+        return V.at[:, (at + (NL - s, s)[d]) % NL]
 
     def value_ring(d, s):
-        line = (b + (NL - s, s)[d]) % NL
+        ref = value_line(b, d, s)
+        return remote(ref, ref, vs.at[d, s], vr.at[d, s], second((b + (1, NL - 1)[d]) % NL), t)
+
+    def value_arrival(d, s):
+        ref = value_line(b, d, s)
         return remote(
-            V.at[line], V.at[line], vs.at[d, s], vr.at[d, s], second((b + (1, NL - 1)[d]) % NL), t
-        )
-
-    def value_arrival(d, s):
-        line = (b + (NL - s, s)[d]) % NL
-        return remote(
-            V.at[line], V.at[line], vs.at[d, s - 1], vr.at[d, s - 1],
-            second((b + (1, NL - 1)[d]) % NL), t,
+            ref, ref, vs.at[d, s - 1], vr.at[d, s - 1], second((b + (1, NL - 1)[d]) % NL), t
         )
 
     def value_share(d, s):
-        line = (z + (NL - s, s)[d]) % NL
-        return remote(V.at[line], V.at[line], gs.at[d, s], gr.at[d, s], sibling, t)
+        ref = value_line(y, d, s)
+        return remote(ref, ref, gs.at[d, s], gr.at[d, s], sibling, t)
 
     value_steps = [(0, 0), (1, 0), (0, 1), (1, 1), (0, 2), (1, 2), (0, 3), (1, 3), (0, 4)]
     value_sent = [p for p in value_steps if p[1] < (4, 3)[p[0]]]
     value_shared = [p for p in value_steps if p != (1, 0)]
 
     def take_value(s):
-        @pl.when(c == 0)
+        @pl.when(c == 1)
         def _():
             for part in value_steps:
                 if part[1] == s:
@@ -354,44 +345,61 @@
                     if part in value_shared:
                         value_share(*part).start()
 
-    @pl.when(c == 0)
+    take(2, (0, 1, 2))
+    x_copies[2].wait_recv()
+    x_copies[3].wait_recv()
+    prepare(left)
+    @pl.when(c == 1)
     def _():
         for k in range(1, NL):
             value_first(k).wait_recv()
 
     take_value(0)
+    take(2, (3,))
+    share(2)
+    prepare(right)
+    def project_stream(stream, lines, fresh=False):
+        def pick(ref, line):
+            return ref[line] if stream == 0 else ref[:, line]
+
+        at = [((z, y)[stream] + k) % NL for k in lines]
+        rows = jnp.concatenate([pick(NT, line).reshape(LINE, -1) for line in at], axis=0)
+        weights = jnp.concatenate(
+            [pick(W.at[stream], line).reshape(LINE, -1) for line in at], axis=0
+        )
+        prod = lax.dot_general(rows, weights, (((0,), (0,)), ((), ())), preferred_element_type=F32)
+        qkv[stream] = prod if fresh else qkv[stream] + prod
+
+    def project(lines, fresh=False):
+        project_stream(0, lines, fresh)
+        project_stream(1, lines, fresh)
+
+    def project_own(lines):
+        each_core(lambda core: project_stream(core, lines))
+
+    def project_other(lines):
+        each_core(lambda core: project_stream(1 - core, lines))
+
+    take(3, (0, 1))
     fwd0.wait_recv()
     fwd1.wait_recv()
     prepare(across)
-
-    def project(one, two, fresh):
-        for stream in range(2):
-            def pick(ref, line, stream=stream):
-                return ref[line] if stream == 0 else ref[:, line]
-
-            at = (z, y)[stream]
-            l0, l1 = (at + one) % NL, (at + two) % NL
-            rows = jnp.concatenate(
-                [pick(NT, l0).reshape(LINE, -1), pick(NT, l1).reshape(LINE, -1)], axis=0
-            )
-            weights = jnp.concatenate(
-                [pick(W.at[stream], l0).reshape(LINE, -1), pick(W.at[stream], l1).reshape(LINE, -1)],
-                axis=0,
-            )
-            prod = lax.dot_general(
-                rows, weights, (((0,), (0,)), ((), ())), preferred_element_type=F32
-            )
-            qkv[stream] = prod if fresh else qkv[stream] + prod
-
     from_other(0)
     from_other(1)
-    project(1, 7, True)
+    project((0, 1, 7), True)
     from_other(2)
-    project(2, 6, False)
-    take(4, order)
+    project((2, 6))
+    take_value(1)
+    take(3, (2, 3))
+    share(3)
+    take(4, range(4))
+    rows_copy = remote(TH.at[1 - c], TH_in, ths, thr, sibling, t)
+    rows_copy.start()
+    project_own((3, 5, 4))
     from_other(3)
-    project(3, 5, False)
-
+    project_other((3, 5))
+
+    take_value(2)
     tab_copy.wait_recv()
     info = []
     for block in range(GEN_BLK):
@@ -414,9 +422,8 @@
             ordered = (pi * BLK + q_in) >= (pj * BLK + k_in)
             allow[i * BLK : (i + 1) * BLK, j * BLK : (j + 1) * BLK] = jnp.where(ordered, meet, 0)
 
-    take_value(1)
     from_other(4)
-    project(0, 4, False)
+    project_other((4,))
 
     loads["cot"].wait()
     keys = qkv[0, :, 2 * HD :].astype(BF16)
@@ -440,44 +447,41 @@
             preferred_element_type=F32,
         )
     vc[...] = total.astype(BF16)
-    take_value(2)
-
-    def sum_copy(i):
-        return remote(Rb.at[i], SR.at[i], ss.at[i], sr.at[i], sibling, t)
-
-    def terms(i, carry):
-        rows = jnp.concatenate(
-            [NT[i + c * (m - i), m + c * (i - m)] for m in range(NL)], axis=0
-        )
-        prod = jnp.dot(rows, vc[...], preferred_element_type=F32).reshape(NL, CHIP, HD)
-        top, bottom = prod[:, :PART, :], prod[:, PART:, :]
-        Rb[i] = jnp.where(c == 0, bottom, top).reshape(NL * PART, HD).astype(BF16)
-        sum_copy(i).start()
-        R[:, pl.ds(pl.multiple_of(i * PART, 8), PART), :] = jnp.where(c == 0, top, bottom)
-        return carry
-
-    lax.fori_loop(0, NL, terms, 0)
-
-    def both_cores(k):
-        line = (a + k) % NL
-        sum_copy(line).wait_recv()
-        return R[line] + SR[line].astype(F32)
-
-    H[4] = both_cores(4).astype(BF16)
+
+    vc_copy = remote(vc, vc_in, vcs, vcr, sibling, t)
+    vc_copy.start()
+    R[...] = jnp.dot(
+        TH[c].reshape(NL * NL * PART, -1), vc[...], preferred_element_type=F32
+    ).reshape(NL, NL * PART, HD)
+    rows_copy.wait_recv()
+    vc_copy.wait_recv()
+
+    def both_cores(ks):
+        lines = [(a + k) % NL for k in ks]
+        rows = jnp.concatenate([TH_in[line].reshape(NL * PART, -1) for line in lines], axis=0)
+        prod = jnp.dot(rows, vc_in[...], preferred_element_type=F32)
+        return [
+            R[line] + prod[i * NL * PART : (i + 1) * NL * PART] for i, line in enumerate(lines)
+        ]
+
+    def sum_copy(k):
+        return remote(H.at[k], P1.at[k], q1s.at[k], q1r.at[k], first((a + k) % NL), t)
+
+    sums = [sum_copy(k) for k in (1, 2, 3, 5, 6, 7)]
     merge = remote(H.at[4], M, ms, mr, first((a + NL - 1) % NL), t)
+    H[4] = both_cores((4,))[0].astype(BF16)
     merge.start()
-    sums = []
-    for k in (3, 2, 6, 5, 1, 7):
-        value = both_cores(k)
-        if k == 5:
-            merge.wait_recv()
-            value = value + M[...].astype(F32)
+    part3, part6, part2 = both_cores((3, 6, 2))
+    for k, value in ((3, part3), (6, part6), (2, part2)):
         H[k] = value.astype(BF16)
-        copy = remote(H.at[k], P1.at[k], q1s.at[k], q1r.at[k], first((a + k) % NL), t)
-        copy.start()
-        sums.append(copy)
-    acc = both_cores(0)
-
+        sum_copy(k).start()
+    part5, part1, part7, acc = both_cores((5, 1, 7, 0))
+    for k, value in ((1, part1), (7, part7)):
+        H[k] = value.astype(BF16)
+        sum_copy(k).start()
+    merge.wait_recv()
+    H[5] = (part5 + M[...].astype(F32)).astype(BF16)
+    sum_copy(5).start()
     take_value(3)
     for copy in sums:
         copy.wait_recv()
@@ -489,9 +493,10 @@
         copy = remote(F.at[(b + k) % NL], P2.at[k], q2s.at[k], q2r.at[k], second((b + k) % NL), t)
         copy.start()
         last.append(copy)
+
     take_value(4)
 
-    @pl.when(c == 1)
+    @pl.when(c == 0)
     def _():
         for part in value_shared:
             value_share(*part).wait_recv()
@@ -515,10 +520,8 @@
         out = out + P2[k]
     grad[...] = out
 
-    for copy in x_copies + sq_copies + sums + last + [sib_copy, tab_copy, fwd0, fwd1, merge]:
+    for copy in x_copies + sq_copies + sums + last + [sib_copy, tab_copy, fwd0, fwd1, rows_copy, vc_copy, merge]:
         copy.wait_send()
-    for i in range(NL):
-        sum_copy(i).wait_send()
     for i in range(7):
         along(i).wait_send()
     for k in range(NL):
@@ -531,9 +534,9 @@
         for s in range(4):
             for d in range(min(s + 1, 2)):
                 to_sibling(core, d, s).wait_send()
-        for j in order:
+        for j in range(4):
             last_to_sibling(core, j).wait_send()
-        if core == 0:
+        if core == 1:
             for k in range(1, NL):
                 value_first(k).wait_send()
             for part in value_sent:
@@ -580,9 +583,11 @@
             pltpu.VMEM((8, rows), F32),
             pltpu.VMEM((3, 8, rows), F32),
             pltpu.VMEM((rows, HD), F32),
+            pltpu.VMEM((2, NL, NT_X, CHIP, rows), BF16),
+            pltpu.VMEM((NL, NT_X, CHIP, rows), BF16),
+            pltpu.VMEM((NL, CHIP, rows), F32),
+            pltpu.VMEM((rows, HD), BF16),
             pltpu.VMEM((NL, NL * PART, HD), F32),
-            pltpu.VMEM((NL, NL * PART, HD), BF16),
-            pltpu.VMEM((NL, NL * PART, HD), BF16),
             pltpu.VMEM((NL, NL * PART, HD), BF16),
             pltpu.VMEM((NL * PART, HD), BF16),
             pltpu.VMEM((NL, NL * PART, HD), BF16),
@@ -599,8 +604,7 @@
             dma((2, 4)), dma((2, 4)),
             dma((2, 4)), dma((2, 4)), dma((4,)), dma((4,)),
             dma((2, 5)), dma((2, 5)),
-            dma((NL,)), dma((NL,)),
-            dma, dma,
+            dma, dma, dma, dma, dma, dma,
             dma((NL,)), dma((NL,)), dma((NL,)), dma((NL,)),
         ],
         compiler_params=pltpu.CompilerParams(

time: 75.5 us -> 71.7 us (0.950)
  Pallas kernels: 71.7 us -> 68.5 us
    pallas_call x1, Pallas kernels: 71.7 us -> 68.5 us  [shards(): pl.pallas_call(kernel, out_shape=(jax.ShapeDtypeStruct((rows, HEADS * HD)...]
where the time goes in v3:
time: 71.7 us; the launch traced here: 71.5 us
  Pallas kernels  68.5 us (96%)
  local copies, waits for them, and re-layouts  2.34 us (3%)
    pallas_call x1, Pallas kernels, shards(): pl.pallas_call(kernel, out_shape=(jax.ShapeDtypeStruct((rows, HEADS * HD)...  68.5 us
    unnamed x4, local copies, waits for them, and re-layouts  2.34 us

profile of v3, /device:TPU:1, one launch (start us, length us, event | category | flops | bytes accessed | tf_op | source)
XLA Modules:
  0.0 71.5 jit_solution(17383825899308892206)
XLA Ops:
  0.6 68.5 %shard_map.104 = (bf16[256,640]{1,0:T(8,128)(2,1)}, f32[40,128]{1,0:T(8,128)}) custom-call(bf16[256,1280]{1,0:T(8,128)(2,1)} %hid.1, bf16[256,640]{1,0:T(8,128)(2,1)} %cot_in.1, f32[4,1,1280]{2,1,0:T(1,128)} %bitcast.1, bf16[40,640]{1,0:T(8,128)(2,1)} %wq_in.1, bf16[40,128]{1,0:T(8,128)(2,1)} %wk_in.1, bf16[40,128]{1,0:T(8,128)(2,1)} %wv_in.1, s32[4]{0:T(128)} %src_in.1, ...), custom_call_target="tpu_custom_call" | custom-call | tf_op jit(solution)/shard_map/pallas_call | solution.py:554
  69.2 0.0 copy-start
  69.2 1.7 %copy.13 = bf16[256,640]{1,0:T(8,128)(2,1)} copy(bf16[256,640]{1,0:T(8,128)(2,1)} %get-tuple-element.4) | data formatting | bytes 655360
  70.9 0.0 copy-done
  70.9 0.6 copy.14
Async XLA Ops:
  69.2 1.7 %copy-start = (f32[40,128]{1,0:T(8,128)S(1)}, f32[40,128]{1,0:T(8,128)}, u32[]{:S(2)}) copy-start(f32[40,128]{1,0:T(8,128)} %get-tuple-element.5) | copy-start | bytes 61444

commit v4 on v3

--- a/solution.py
+++ b/solution.py
@@ -32,10 +32,10 @@
     att, grad,
     cot, gain, wq, wk, wv, src, seg, pos,
     W, V, X, NT, stage, sib, tab_out, tab_in, qkv, probs, allow, vc, sq_out, sq_in, scale,
-    TH, TH_in, top_rows, vc_in, R, H, M, P1, F, P2,
+    TH, TH_in, top_rows, vc_in, R, H, P1, F, P2, own_item,
     ld, sib_s, sib_r, tab_s, tab_r, xs, xr, xfs, xfr,
     sqs, sqr, p1s, p1r, v1s, v1r, os, rs, rr, vs, vr, fs, fr, f4s, f4r, gs, gr,
-    ths, thr, vcs, vcr, ms, mr, q1s, q1r, q2s, q2r,
+    ths, thr, vcs, vcr, q1s, q1r, q2s, q2r,
 ):
     g = lax.axis_index("fsdp")
     t = lax.axis_index("tp")
@@ -280,6 +280,8 @@
         for k in (1, 7, 2, 6, 3, 5, 4):
             value_first(k).start()
 
+    take(1, (1,))
+
     x_copies[0].wait_recv()
     fwd0 = remote(X.at[left, 0], X.at[left, 0], xfs.at[0], xfr.at[0], g, right)
     fwd0.start()
@@ -308,7 +310,6 @@
         TH[0, :, s] = top_rows[...].astype(BF16)
 
     loads["gain"].wait()
-    take(1, (1,))
     prepare(t)
     take(1, (2, 3))
     share(1)
@@ -467,27 +468,25 @@
     def sum_copy(k):
         return remote(H.at[k], P1.at[k], q1s.at[k], q1r.at[k], first((a + k) % NL), t)
 
-    sums = [sum_copy(k) for k in (1, 2, 3, 5, 6, 7)]
-    merge = remote(H.at[4], M, ms, mr, first((a + NL - 1) % NL), t)
-    H[4] = both_cores((4,))[0].astype(BF16)
-    merge.start()
-    part3, part6, part2 = both_cores((3, 6, 2))
-    for k, value in ((3, part3), (6, part6), (2, part2)):
-        H[k] = value.astype(BF16)
-        sum_copy(k).start()
-    part5, part1, part7, acc = both_cores((5, 1, 7, 0))
+    sums = [sum_copy(k) for k in range(1, NL)]
+    for ks in ((4,), (3, 5), (2, 6)):
+        for k, value in zip(ks, both_cores(ks)):
+            H[k] = value.astype(BF16)
+            sum_copy(k).start()
+    part1, part7, acc = both_cores((1, 7, 0))
     for k, value in ((1, part1), (7, part7)):
         H[k] = value.astype(BF16)
         sum_copy(k).start()
-    merge.wait_recv()
-    H[5] = (part5 + M[...].astype(F32)).astype(BF16)
-    sum_copy(5).start()
     take_value(3)
     for copy in sums:
         copy.wait_recv()
-    for k in (1, 2, 3, 5, 6, 7):
+    for k in range(1, NL):
         acc = acc + P1[k].astype(F32)
-    F[...] = acc.reshape(NL, PART, HD)
+    items = acc.reshape(NL, PART, HD)
+    F[...] = jnp.concatenate([items, items[:, :8]], axis=1).astype(BF16)
+    own_item[...] = jnp.sum(
+        jnp.where(lax.broadcasted_iota(jnp.int32, (NL, 1, 1), 0) == b, items, 0.0), axis=0
+    )
     last = []
     for k in (4, 3, 5, 2, 6, 1, 7):
         copy = remote(F.at[(b + k) % NL], P2.at[k], q2s.at[k], q2r.at[k], second((b + k) % NL), t)
@@ -513,14 +512,7 @@
             probs[head], values, preferred_element_type=F32
         ).astype(BF16)
 
-    for copy in last:
-        copy.wait_recv()
-    out = F[b]
-    for k in range(1, NL):
-        out = out + P2[k]
-    grad[...] = out
-
-    for copy in x_copies + sq_copies + sums + last + [sib_copy, tab_copy, fwd0, fwd1, rows_copy, vc_copy, merge]:
+    for copy in x_copies + sq_copies + sums + [sib_copy, tab_copy, fwd0, fwd1, rows_copy, vc_copy]:
         copy.wait_send()
     for i in range(7):
         along(i).wait_send()
@@ -546,12 +538,44 @@
 
     each_core(all_left)
 
+    for copy in last:
+        copy.wait_recv()
+    out = own_item[...]
+    for k in range(1, NL):
+        out = out + P2[k].astype(F32)[:PART]
+    grad[...] = out
+
+    for copy in last:
+        copy.wait_send()
+
+
+def hand_over(att, grad, att_out, grad_out, att_held, grad_held, read, write):
+    whole = pl.ds(0, PART)
+    pieces = [(grad, grad_held, grad_out, whole)]
+    for i in range(4):
+        pieces.append((att, att_held, att_out, pl.ds(64 * i, 64)))
+    reads = [
+        pltpu.make_async_copy(source.at[rows], held.at[rows], read.at[i])
+        for i, (source, held, _, rows) in enumerate(pieces)
+    ]
+    writes = [
+        pltpu.make_async_copy(held.at[rows], target.at[rows], write.at[i])
+        for i, (_, held, target, rows) in enumerate(pieces)
+    ]
+    for copy in reads:
+        copy.start()
+    for one, two in zip(reads, writes):
+        one.wait()
+        two.start()
+    for copy in writes:
+        copy.wait()
+
 
 def shards(hidden_rows, cotangent, norm_gain, query_weight, key_weight, value_weight, source, segment, position):
     rows = GEN_BLK * BLK
     vmem = pl.BlockSpec(memory_space=pltpu.VMEM)
     dma = pltpu.SemaphoreType.DMA
-    return pl.pallas_call(
+    made = pl.pallas_call(
         kernel,
         out_shape=(
             jax.ShapeDtypeStruct((rows, HEADS * HD), BF16),
@@ -589,10 +613,10 @@
             pltpu.VMEM((rows, HD), BF16),
             pltpu.VMEM((NL, NL * PART, HD), F32),
             pltpu.VMEM((NL, NL * PART, HD), BF16),
-            pltpu.VMEM((NL * PART, HD), BF16),
             pltpu.VMEM((NL, NL * PART, HD), BF16),
-            pltpu.VMEM((NL, PART, HD), F32),
-            pltpu.VMEM((NL, PART, HD), F32),
+            pltpu.VMEM((NL, PART + 8, HD), BF16),
+            pltpu.VMEM((NL, PART + 8, HD), BF16),
+            pltpu.VMEM((PART, HD), F32),
             dma((10,)),
             dma, dma, dma, dma,
             dma((2, 2)), dma((2, 2)), dma((2,)), dma((2,)),
@@ -604,7 +628,7 @@
             dma((2, 4)), dma((2, 4)),
             dma((2, 4)), dma((2, 4)), dma((4,)), dma((4,)),
             dma((2, 5)), dma((2, 5)),
-            dma, dma, dma, dma, dma, dma,
+            dma, dma, dma, dma,
             dma((NL,)), dma((NL,)), dma((NL,)), dma((NL,)),
         ],
         compiler_params=pltpu.CompilerParams(
@@ -614,6 +638,20 @@
         hidden_rows, cotangent, norm_gain.reshape(NT_X, 1, SLICE), query_weight, key_weight, value_weight,
         source, segment, position,
     )
+    hbm = pl.BlockSpec(memory_space=pltpu.HBM)
+    return pl.pallas_call(
+        hand_over,
+        out_shape=tuple(jax.ShapeDtypeStruct(one.shape, one.dtype) for one in made),
+        in_specs=[hbm, hbm],
+        out_specs=(hbm, hbm),
+        scratch_shapes=[
+            pltpu.VMEM(made[0].shape, BF16),
+            pltpu.VMEM(made[1].shape, F32),
+            dma((5,)),
+            dma((5,)),
+        ],
+        compiler_params=pltpu.CompilerParams(vmem_limit_bytes=60 * 1024 * 1024),
+    )(*made)
 
 
 def solution(mesh):

time: 71.7 us -> 71.1 us (level)
  local copies, waits for them, and re-layouts: 2.34 us -> 0 us
  Pallas kernels: 68.5 us -> 70.1 us
    unnamed x4 -> x0, local copies, waits for them, and re-layouts: 2.34 us -> none
    pallas_call x0 -> x1, Pallas kernels: none -> 1.74 us  [shards(): pl.pallas_call(hand_over, out_shape=tuple((jax.ShapeDtypeStruct(one.shape...]
where the time goes in v4:
time: 71.1 us; the launch traced here: 70.9 us
  Pallas kernels  70.1 us (99%)
  between operations  0.8 us (1%)
    pallas_call x1, Pallas kernels, shards(): pl.pallas_call(kernel, out_shape=(jax.ShapeDtypeStruct((rows, HEADS * HD)...  68.3 us
    pallas_call x1, Pallas kernels, shards(): pl.pallas_call(hand_over, out_shape=tuple((jax.ShapeDtypeStruct(one.shape...  1.74 us

profile of v4, /device:TPU:1, one launch (start us, length us, event | category | flops | bytes accessed | tf_op | source)
XLA Modules:
  0.0 70.9 jit_solution(14044131580703024182)
XLA Ops:
  0.6 68.3 %shard_map.104 = (bf16[256,640]{1,0:T(8,128)(2,1)}, f32[40,128]{1,0:T(8,128)}) custom-call(bf16[256,1280]{1,0:T(8,128)(2,1)} %hid.1, bf16[256,640]{1,0:T(8,128)(2,1)} %cot_in.1, f32[4,1,1280]{2,1,0:T(1,128)} %bitcast.1, bf16[40,640]{1,0:T(8,128)(2,1)} %wq_in.1, bf16[40,128]{1,0:T(8,128)(2,1)} %wk_in.1, bf16[40,128]{1,0:T(8,128)(2,1)} %wv_in.1, s32[4]{0:T(128)} %src_in.1, ...), custom_call_target="tpu_custom_call" | custom-call | tf_op jit(solution)/shard_map/pallas_call | solution.py:578
  69.0 1.7 %shard_map.105 = (bf16[256,640]{1,0:T(8,128)(2,1)}, f32[40,128]{1,0:T(8,128)}) custom-call(bf16[256,640]{1,0:T(8,128)(2,1)} %get-tuple-element.4.att, f32[40,128]{1,0:T(8,128)} %get-tuple-element.5.grad), custom_call_target="tpu_custom_call" | custom-call | tf_op jit(solution)/shard_map/pallas_call | solution.py:642

commit v5 on v4

--- a/solution.py
+++ b/solution.py
@@ -400,7 +400,6 @@
     from_other(3)
     project_other((3, 5))
 
-    take_value(2)
     tab_copy.wait_recv()
     info = []
     for block in range(GEN_BLK):
@@ -454,6 +453,7 @@
     R[...] = jnp.dot(
         TH[c].reshape(NL * NL * PART, -1), vc[...], preferred_element_type=F32
     ).reshape(NL, NL * PART, HD)
+    take_value(2)
     rows_copy.wait_recv()
     vc_copy.wait_recv()
 

time: 71.1 us -> 71.7 us (level)
  no operation moved by 1% of the time
where the time goes in v5:
time: 71.7 us; the launch traced here: 71.1 us
  Pallas kernels  70.3 us (98%)
  between operations  0.8 us (1%)
    pallas_call x1, Pallas kernels, shards(): pl.pallas_call(kernel, out_shape=(jax.ShapeDtypeStruct((rows, HEADS * HD)...  68.5 us
    pallas_call x1, Pallas kernels, shards(): pl.pallas_call(hand_over, out_shape=tuple((jax.ShapeDtypeStruct(one.shape...  1.74 us

profile of v5, /device:TPU:1, one launch (start us, length us, event | category | flops | bytes accessed | tf_op | source)
XLA Modules:
  0.0 71.1 jit_solution(2398684807051633385)
XLA Ops:
  0.6 68.5 %shard_map.104 = (bf16[256,640]{1,0:T(8,128)(2,1)}, f32[40,128]{1,0:T(8,128)}) custom-call(bf16[256,1280]{1,0:T(8,128)(2,1)} %hid.1, bf16[256,640]{1,0:T(8,128)(2,1)} %cot_in.1, f32[4,1,1280]{2,1,0:T(1,128)} %bitcast.1, bf16[40,640]{1,0:T(8,128)(2,1)} %wq_in.1, bf16[40,128]{1,0:T(8,128)(2,1)} %wk_in.1, bf16[40,128]{1,0:T(8,128)(2,1)} %wv_in.1, s32[4]{0:T(128)} %src_in.1, ...), custom_call_target="tpu_custom_call" | custom-call | tf_op jit(solution)/shard_map/pallas_call | solution.py:578
  69.2 1.7 %shard_map.105 = (bf16[256,640]{1,0:T(8,128)(2,1)}, f32[40,128]{1,0:T(8,128)}) custom-call(bf16[256,640]{1,0:T(8,128)(2,1)} %get-tuple-element.4.att, f32[40,128]{1,0:T(8,128)} %get-tuple-element.5.grad), custom_call_target="tpu_custom_call" | custom-call | tf_op jit(solution)/shard_map/pallas_call | solution.py:642
